TPU v7x, 128 devices: a whole 4x4x4 slice. The times are simulated.
128 devices in a mesh: lat: 16 (over x, y_lo, core), lon: 8 (over z, y_hi).
Axes of the slice: x: 4, y: 4 (y_hi: 2, y_lo: 2; y = y_hi * 2 + y_lo), z: 4, core: 2. Of those that a mesh axis runs over, the one named last changes fastest.
Arguments:
- ocean_state: float32 [100, 128, 1024], P(None, 'lat', 'lon'), may hold values from -6 to 6
- ocean_mask: int32 [128, 1024], P('lat', 'lon'), may hold values from 0 to 1, as said below
- cotangent: float32 [100, 128, 1024], P(None, 'lat', 'lon'), may hold values from -6 to 6
- encoder_weight: bfloat16 [200, 100], replicated, may hold values from -0.625 to 0.625
- encoder_bias: float32 [200], replicated, may hold values from -3 to 3
- depth_weight: float32 [200, 7, 7], replicated, may hold values from -0.875 to 0.875
- norm_gain: float32 [200], replicated, may hold values from 0.25 to 1.75
- up_weight: bfloat16 [800, 200], replicated, may hold values from -0.4375 to 0.4375
- down_weight: bfloat16 [200, 800], replicated, may hold values from -0.21875 to 0.21875
- decoder_weight: bfloat16 [100, 200], replicated, may hold values from -0.4375 to 0.4375
Outputs:
- state_grad: float32 [100, 128, 1024], P(None, 'lat', 'lon')
- up_grad: float32 [800, 200], replicated
- down_grad: float32 [200, 800], replicated
- depth_grad: float32 [200, 7, 7], replicated
Inputs may be any that keep to these rules, and one draw needn't show every extreme that they name: `ocean_mask`: 1 marks an ocean cell, 0 a land cell.
All inputs are finite; a program needn't handle non-finite values.
Results may differ from a plain program's by a relative error of at most 0.012.
Values may be sent and summed in bfloat16 or wider, within the bound.
A program may use at most 128 MiB of HBM per device.

v0:
```python
import math

import jax
import jax.numpy as jnp
import numpy as np
from jax import lax
from jax.experimental import pallas as pl
from jax.experimental.pallas import tpu as pltpu
from jax.sharding import PartitionSpec as P

EPSILON = 1e-06
GELU_SCALE = 0.7978845608028654
GELU_CUBE = 0.044715
MESH = pl.DeviceIdType.MESH
F32 = jnp.float32
BF16 = jnp.bfloat16
LEVELS = 100
WIDTH = 200
HIDDEN = 800
ROWS = 8
COLS = 128
CHUNKS = 4
SPAN = 256
BLOCKS = WIDTH // 8

STEPS = ((1, 0), (-1, 0), (0, 1), (0, -1), (1, 1), (1, -1), (-1, 1), (-1, -1))
LINES = {2: (16, 16, 32), 3: (80, 80, 32), 4: (48, 0, 16), 5: (112, 64, 16), 6: (0, 48, 16), 7: (64, 112, 16)}


def edge_tables():
    pack = np.zeros((ROWS * COLS, 128), np.float32)
    spread = np.zeros((128, 14 * COLS), np.float32)
    for side in range(2):
        for first, rows, sent, filled in ((0, 3, 0, 0), (16, 8, 0, 3), (48, 3, 5, 11)):
            for q in range(3 * rows):
                row, k = q // 3, q % 3
                line = 64 * side + first + q
                pack[COLS * (sent + row) + (k if side else 125 + k), line] = 1.0
                spread[line, COLS * (filled + row) + (k if side else 125 + k)] = 1.0
    return pack.astype(jnp.bfloat16), spread.astype(jnp.bfloat16)


def dot(a, b):
    return jnp.dot(a, b, preferred_element_type=F32)


def dot_nt(a, b):
    return lax.dot_general(a, b, (((1,), (1,)), ((), ())), preferred_element_type=F32)


def gelu_parts(p):
    square = p * p
    half = 0.5 * jnp.tanh(p * (GELU_SCALE + (GELU_SCALE * GELU_CUBE) * square)) + 0.5
    value = p * half
    slope = half + value * (1.0 - half) * (2.0 * GELU_SCALE + (6.0 * GELU_SCALE * GELU_CUBE) * square)
    return value, slope


def rows_of(value):
    return value[:, :COLS], value[:, COLS:]


def pair(ref, k):
    return jnp.concatenate([ref[2 * k], ref[2 * k + 1]], axis=1)


def main_kernel(
    state, mask, cot, encw, params, upw, downw, decw, pack, spread,
    out, up_out, down_out, depth_out,
    taps, pad_one, side_one, pad_two, side_two, pad_g, side_g, grad, conv, std_one, std_two, inv_one, inv_two,
    act_one, slope_one, normed_one, normed_two, join, grad_mid, depth_acc,
    upt, downt, dect, enct, own, edge_rows, line_out, line_in, send_sem, recv_sem,
):
    lat, lon = lax.axis_index("lat"), lax.axis_index("lon")
    lats, lons = lax.axis_size("lat"), lax.axis_size("lon")
    has_north, has_south = lat > 0, lat < lats - 1
    north, south = lat - 1, lat + 1
    east, west = lax.rem(lon + 1, lons), lax.rem(lon + lons - 1, lons)
    lat_of = {0: lat, 1: south, -1: north}
    lon_of = {0: lon, 1: east, -1: west}

    def when_lat(step, run):
        if step == 0:
            run()
        elif step > 0:
            pl.when(has_south)(run)
        else:
            pl.when(has_north)(run)

    barrier = pltpu.get_barrier_semaphore()
    for step_lat, step_lon in STEPS:
        when_lat(step_lat, lambda a=step_lat, b=step_lon: pl.semaphore_signal(
            barrier, inc=1, device_id=(lat_of[a], lon_of[b]), device_id_type=MESH))

    def copy_of(turn, m):
        if m == 0:
            src, dst = own.at[turn, pl.ds(5, 3)], edge_rows.at[turn, 0]
        elif m == 1:
            src, dst = own.at[turn, pl.ds(0, 3)], edge_rows.at[turn, 1]
        else:
            first, filled, count = LINES[m]
            src, dst = line_out.at[turn, pl.ds(first, count)], line_in.at[turn, pl.ds(filled, count)]
        return pltpu.make_async_remote_copy(
            src_ref=src, dst_ref=dst, send_sem=send_sem.at[turn, m], recv_sem=recv_sem.at[turn, m],
            device_id=(lat_of[STEPS[m][0]], lon_of[STEPS[m][1]]), device_id_type=MESH)

    def send_halo(turn):
        for m in (0, 1):
            when_lat(STEPS[m][0], lambda m=m: copy_of(turn, m).start())
        flat = jnp.concatenate([own[turn, r] for r in range(ROWS)], axis=1)
        picked = dot(flat, pack[...])
        picked = jnp.concatenate([picked, jnp.zeros((48, 128), F32)], axis=0)
        line_out[turn] = picked.T.astype(BF16)
        for m in range(2, 8):
            when_lat(STEPS[m][0], lambda m=m: copy_of(turn, m).start())

    def take_halo(turn, pad, side):
        for m in range(8):
            when_lat(-STEPS[m][0], lambda m=m: copy_of(turn, m).wait_recv())
        for r in range(3):
            pad[r] = edge_rows[turn, 0, r].astype(F32)[:WIDTH]
            pad[11 + r] = edge_rows[turn, 1, r].astype(F32)[:WIDTH]
        lines = line_in[turn].astype(F32).T[:WIDTH].astype(BF16)
        wide = dot(lines, spread[...])
        for r in range(14):
            side[r] = wide[:, COLS * r : COLS * (r + 1)]

    def keep(turn, k, value, pad):
        rounded = value.astype(BF16)
        again = rounded.astype(F32)
        filled = jnp.concatenate([value, jnp.zeros((8, SPAN), F32)], axis=0).astype(BF16)
        for q in range(2):
            pad[3 + 2 * k + q] = again[:, COLS * q : COLS * (q + 1)]
            own[turn, 2 * k + q] = filled[:, COLS * q : COLS * (q + 1)]
        return again

    lane = lax.broadcasted_iota(jnp.int32, (14, 8, COLS), 2)

    def shifted(main, edge, s):
        if s == 0:
            return main
        if s > 0:
            return pltpu.roll(jnp.where(lane < s, edge, main), COLS - s, 2)
        return pltpu.roll(jnp.where(lane >= COLS + s, edge, main), -s, 2)

    def depthwise(pad, side, target, adjoint):
        def block(b, carry):
            at = pl.ds(pl.multiple_of(8 * b, 8), 8)
            main, edge = pad[:, at, :], side[:, at, :]
            total = jnp.zeros((ROWS, 8, COLS), F32)
            for j in range(7):
                moved = shifted(main, edge, 3 - j if adjoint else j - 3)
                for i in range(7):
                    first = 6 - i if adjoint else i
                    total = total + taps[7 * i + j, at, :][None] * moved[first : first + ROWS]
            target[:, at, :] = total
            return carry
        lax.fori_loop(0, BLOCKS, block, 0)

    def depth_terms(pad, side, fresh):
        def block(b, carry):
            at = pl.ds(pl.multiple_of(8 * b, 8), 8)
            main, edge, slope = pad[:, at, :], side[:, at, :], grad[:, at, :]
            for j in range(7):
                moved = shifted(main, edge, j - 3)
                for i in range(7):
                    term = jnp.sum(slope * moved[i : i + ROWS], axis=0)
                    if fresh:
                        depth_acc[7 * i + j, at, :] = term
                    else:
                        depth_acc[7 * i + j, at, :] += term
            return carry
        lax.fori_loop(0, BLOCKS, block, 0)

    def over_chunks(body):
        lax.fori_loop(0, CHUNKS, lambda k, c: (body(k), c)[1], 0)

    def mask_of(k):
        both = jnp.concatenate([mask[pl.ds(2 * k, 1), :], mask[pl.ds(2 * k + 1, 1), :]], axis=1)
        return both.astype(F32)

    def levels_of(ref, k):
        return jnp.concatenate(
            [ref[pl.ds(2 * k + q, LEVELS, stride=ROWS), :] for q in range(2)], axis=1)

    bias = params[:, 49:50]
    gain = params[:, 50:51]

    def encode(k, value, turn, pad):
        keep(turn, k, dot(encw[...], value.astype(BF16)) + bias, pad)

    over_chunks(lambda k: encode(k, levels_of(state, k), 0, pad_one))

    def ends(turn):
        @pl.when(jnp.logical_not(has_north))
        def _():
            edge_rows[turn, 0] = jnp.zeros_like(edge_rows[turn, 0])
            for part in (0, 64):
                line_in[turn, pl.ds(part, 16)] = jnp.zeros((16, SPAN), BF16)

        @pl.when(jnp.logical_not(has_south))
        def _():
            edge_rows[turn, 1] = jnp.zeros_like(edge_rows[turn, 1])
            for part in (48, 112):
                line_in[turn, pl.ds(part, 16)] = jnp.zeros((16, SPAN), BF16)

    peers = 2 + 3 * jnp.minimum(lat, 1) + 3 * jnp.minimum(lats - 1 - lat, 1)
    pl.semaphore_wait(barrier, peers)
    send_halo(0)

    for turn in range(4):
        ends(turn)
    for t in range(49):
        taps[t] = jnp.broadcast_to(params[:, t : t + 1], (WIDTH, COLS))
    upt[...] = upw[...].astype(F32).T.astype(BF16)
    downt[...] = downw[...].astype(F32).T.astype(BF16)
    dect[...] = decw[...].astype(F32).T.astype(BF16)
    enct[...] = encw[...].astype(F32).T.astype(BF16)

    take_halo(0, pad_one, side_one)
    depthwise(pad_one, side_one, conv, False)

    def normalize(k, std, inv, normed):
        value = pair(conv, k)
        centre = value - jnp.sum(value, axis=0, keepdims=True) * (1.0 / WIDTH)
        inverse = lax.rsqrt(jnp.sum(centre * centre, axis=0, keepdims=True) * (1.0 / WIDTH) + EPSILON)
        standard = centre * inverse
        std[2 * k], std[2 * k + 1] = rows_of(standard)
        inv[k] = jnp.broadcast_to(inverse, (8, SPAN))
        result = (standard * gain).astype(BF16)
        normed[k] = result
        return result

    def forward(k):
        ocean = mask_of(k)
        preact = dot(upw[...], normalize(k, std_one, inv_one, normed_one))
        value, slope = gelu_parts(preact)
        value = value.astype(BF16)
        act_one[k] = value
        slope_one[k] = slope.astype(BF16)
        features = jnp.concatenate([pad_one[3 + 2 * k], pad_one[4 + 2 * k]], axis=1)
        joined = (features + ocean * dot(downw[...], value)).astype(BF16)
        middle = levels_of(state, k) + ocean * dot(decw[...], joined)
        encode(k, middle, 1, pad_two)

    over_chunks(forward)
    send_halo(1)
    take_halo(1, pad_two, side_two)
    depthwise(pad_two, side_two, conv, False)

    def reverse(k, turn, upstream, normed, value, slope, std, inv, fresh):
        ocean = mask_of(k)
        grad_join = dot(dect[...], (ocean * upstream).astype(BF16))
        join[k] = grad_join
        grad_branch = (ocean * grad_join).astype(BF16)
        grad_pre = (dot(downt[...], grad_branch) * slope).astype(BF16)
        grad_norm = dot(upt[...], grad_pre)
        up_term = dot_nt(grad_pre, normed)
        down_term = dot_nt(value, grad_branch)
        if fresh:
            @pl.when(k == 0)
            def _():
                up_out[...] = up_term
                down_out[...] = down_term

            @pl.when(k > 0)
            def _():
                up_out[...] += up_term
                down_out[...] += down_term
        else:
            up_out[...] += up_term
            down_out[...] += down_term
        standard = pair(std, k)
        grad_hat = grad_norm * gain
        first = jnp.sum(grad_hat, axis=0, keepdims=True) * (1.0 / WIDTH)
        second = jnp.sum(grad_hat * standard, axis=0, keepdims=True) * (1.0 / WIDTH)
        result = inv[k][0:1] * (grad_hat - first - standard * second)
        grad[2 * k], grad[2 * k + 1] = rows_of(result)
        keep(turn, k, result, pad_g)

    def late(k):
        normed = normalize(k, std_two, inv_two, normed_two)
        value, slope = gelu_parts(dot(upw[...], normed))
        reverse(k, 2, levels_of(cot, k), normed, value.astype(BF16), slope, std_two, inv_two, True)

    over_chunks(late)
    send_halo(2)
    depth_terms(pad_two, side_two, True)
    take_halo(2, pad_g, side_g)
    depthwise(pad_g, side_g, conv, True)

    def early(k):
        grad_input = (join[k] + pair(conv, k)).astype(BF16)
        upstream = levels_of(cot, k) + dot(enct[...], grad_input)
        grad_mid[k] = upstream
        reverse(k, 3, upstream, normed_one[k], act_one[k], slope_one[k].astype(F32), std_one, inv_one, False)

    over_chunks(early)
    send_halo(3)
    depth_terms(pad_one, side_one, False)
    take_halo(3, pad_g, side_g)
    depthwise(pad_g, side_g, conv, True)

    def last(k):
        grad_input = (join[k] + pair(conv, k)).astype(BF16)
        result = grad_mid[k] + dot(enct[...], grad_input)
        for q in range(2):
            out[pl.ds(2 * k + q, LEVELS, stride=ROWS), :] = result[:, COLS * q : COLS * (q + 1)]

    over_chunks(last)
    column = lax.broadcasted_iota(jnp.int32, (WIDTH, COLS), 1)
    picked = jnp.zeros((WIDTH, COLS), F32)
    for t in range(49):
        picked = jnp.where(column == t, jnp.sum(depth_acc[t], axis=1, keepdims=True), picked)
    depth_out[...] = picked
    for turn in range(4):
        for m in range(8):
            when_lat(STEPS[m][0], lambda m=m: copy_of(turn, m).wait_send())


def main_call(*operands):
    vmem = pl.BlockSpec(memory_space=pltpu.VMEM)
    padded = pltpu.VMEM((14, WIDTH, COLS), F32)
    plane = pltpu.VMEM((ROWS, WIDTH, COLS), F32)
    return pl.pallas_call(
        main_kernel,
        out_shape=[
            jax.ShapeDtypeStruct((LEVELS * ROWS, COLS), F32),
            jax.ShapeDtypeStruct((HIDDEN, WIDTH), F32),
            jax.ShapeDtypeStruct((HIDDEN, WIDTH), F32),
            jax.ShapeDtypeStruct((WIDTH, COLS), F32),
        ],
        in_specs=[vmem] * len(operands),
        out_specs=[vmem] * 4,
        scratch_shapes=[
            pltpu.VMEM((49, WIDTH, COLS), F32),
            padded, padded, padded, padded, padded, padded,
            plane, plane, plane, plane,
            pltpu.VMEM((CHUNKS, 8, SPAN), F32),
            pltpu.VMEM((CHUNKS, 8, SPAN), F32),
            pltpu.VMEM((CHUNKS, HIDDEN, SPAN), BF16),
            pltpu.VMEM((CHUNKS, HIDDEN, SPAN), BF16),
            pltpu.VMEM((CHUNKS, WIDTH, SPAN), BF16),
            pltpu.VMEM((CHUNKS, WIDTH, SPAN), BF16),
            pltpu.VMEM((CHUNKS, WIDTH, SPAN), F32),
            pltpu.VMEM((CHUNKS, LEVELS, SPAN), F32),
            pltpu.VMEM((49, WIDTH, COLS), F32),
            pltpu.VMEM((WIDTH, HIDDEN), BF16),
            pltpu.VMEM((HIDDEN, WIDTH), BF16),
            pltpu.VMEM((WIDTH, LEVELS), BF16),
            pltpu.VMEM((LEVELS, WIDTH), BF16),
            pltpu.VMEM((4, ROWS, 208, COLS), BF16),
            pltpu.VMEM((4, 2, 3, 208, COLS), BF16),
            pltpu.VMEM((4, 128, SPAN), BF16),
            pltpu.VMEM((4, 128, SPAN), BF16),
            pltpu.SemaphoreType.DMA((4, 8)),
            pltpu.SemaphoreType.DMA((4, 8)),
        ],
        compiler_params=pltpu.CompilerParams(
            collective_id=0, has_side_effects=True, vmem_limit_bytes=58 * 1024 * 1024),
    )(*operands)


def per_device(
    ocean_state, ocean_mask, cotangent, encoder_weight, encoder_bias, depth_weight,
    norm_gain, up_weight, down_weight, decoder_weight,
):
    total_rows = ROWS * lax.axis_size("lat")
    total_cols = COLS * lax.axis_size("lon")
    params = jnp.concatenate(
        [depth_weight.reshape(WIDTH, 49), encoder_bias[:, None], norm_gain[:, None], jnp.zeros((WIDTH, 77), F32)],
        axis=1)
    pack, spread = edge_tables()
    state_grad, up_sum, down_sum, depth_sum = main_call(
        ocean_state.reshape(LEVELS * ROWS, COLS), ocean_mask, cotangent.reshape(LEVELS * ROWS, COLS),
        encoder_weight, params, up_weight, down_weight, decoder_weight,
        jnp.asarray(pack), jnp.asarray(spread))
    joined = jnp.concatenate([up_sum, down_sum, jnp.pad(depth_sum, ((0, 0), (0, WIDTH - COLS)))], axis=0)
    summed = lax.psum(joined, ("lat", "lon")) * (1.0 / math.sqrt(total_rows * total_cols))
    return (
        state_grad.reshape(ocean_state.shape),
        summed[:HIDDEN],
        summed[HIDDEN : 2 * HIDDEN].T,
        summed[2 * HIDDEN :, :49].reshape(WIDTH, 7, 7),
    )


def solution(mesh):
    return jax.shard_map(
        per_device,
        mesh=mesh,
        in_specs=(
            P(None, "lat", "lon"), P("lat", "lon"), P(None, "lat", "lon"),
            P(), P(), P(), P(), P(), P(), P(),
        ),
        out_specs=(P(None, "lat", "lon"), P(), P(), P()),
        check_vma=False,
    )
```

profile of v0, /device:TPU:1, one launch (start us, length us, event | category | flops | bytes accessed | tf_op | source)
XLA Modules:
  0.0 254.8 jit_solution(1473093692115372599)
XLA Ops:
  7.2 0.0 all-reduce.3.cloned.1.call-start
  7.2 1.5 copy.26.decw
  8.7 0.8 reshape.25
  9.6 0.1 copy.22
  9.7 0.8 copy.23
  10.5 0.8 copy.24
  11.3 1.9 copy.25.upw
  13.2 0.1 pad.11.clone
  13.3 0.8 maximum_maximum_fusion.params
  14.1 78.4 %shard_map.147 = (f32[800,128]{1,0:T(8,128)}, f32[800,200]{1,0:T(8,128)}, f32[800,200]{1,0:T(8,128)}, f32[200,128]{1,0:T(8,128)}) custom-call(f32[800,128]{1,0:T(8,128)} %bitcast.11, s32[8,128]{1,0:T(8,128)} %mask.1, f32[800,128]{1,0:T(8,128)} %bitcast.12, bf16[200,100]{1,0:T(8,128)(2,1)} %encw.1, f32[200,128]{1,0:T(8,128)} %maximum_maximum_fusion.params, ...), custom_call_target="tpu_custom_call" | custom-call | tf_op jit(solution)/shard_map/pallas_call | solution.py:325
  92.4 2.8 %select_maximum_fusion = f32[1800,200]{1,0:T(8,128)} fusion(f32[200,128]{1,0:T(8,128)} %get-tuple-element.11, f32[800,200]{1,0:T(8,128)} %get-tuple-element.10, f32[800,200]{1,0:T(8,128)} %get-tuple-element.9), kind=kLoop, calls=%fused_computation | loop fusion | flops 1440000 | bytes 2822400 | tf_op jit(solution)/shard_map/concatenate | solution.py:378
  95.3 0.0 all-reduce.3.cloned.1.call-update
  95.3 147.1 %all-reduce.3.cloned.1.call-done = f32[1800,200]{1,0:T(8,128)} async-done(((f32[1800,200]{1,0:T(8,128)}), f32[1800,200]{1,0:T(8,128)}) %all-reduce.3.cloned.1.call-update) | async-done | bytes 1440016 | tf_op jit(solution)/shard_map/psum | solution.py:379
  242.3 1.7 broadcast_multiply_fusion
  244.0 0.1 slice_bitcast_fusion
  244.1 0.0 copy-start
  244.2 0.1 copy.27
  244.2 0.6 reshape.27
  244.9 1.1 copy.29
  246.0 1.1 copy.28
  247.2 0.0 copy-done
  247.2 0.8 copy.32
  (2 shorter events, 0.0 us)
Async XLA Ops:
  7.2 235.2 %all-reduce.3.cloned.1.call-start = ((), (), s32[]{:S(2)}) async-start(), calls=%async_computation | async-start | bytes 3686400 | tf_op jit(solution)/shard_map/psum | solution.py:379
  244.1 3.0 %copy-start = (f32[800,128]{1,0:T(8,128)S(1)}, f32[800,128]{1,0:T(8,128)}, u32[]{:S(2)}) copy-start(f32[800,128]{1,0:T(8,128)} %get-tuple-element.8) | copy-start | bytes 1228804
Sparse Core Ops, SparseCore 0:
  95.4 146.8 all-reduce.2
where the time goes:
time: 255 us
  waiting for transfers between devices  147 us (58%)
  Pallas kernels  78.4 us (31%)
  between operations  14.1 us (6%)
  local copies, waits for them, and re-layouts  9.95 us (4%)
  other arithmetic  5.26 us (2%)
    psum x1, waiting for transfers between devices, per_device(): lax.psum(joined, ('lat', 'lon'))  147 us
    pallas_call x1, Pallas kernels, main_call(): pl.pallas_call(main_kernel, out_shape=[jax.ShapeDtypeStruct((LEVELS * ROW...  78.4 us
    unnamed x7, local copies, waits for them, and re-layouts  6.5 us
  transfers between devices with their start and end apart: 1, of which 1 were waited for; matrix products, arithmetic and copies ran while one was open for 0% of the time, Pallas kernels for 0%

commit v1 on v0

--- a/solution.py
+++ b/solution.py
@@ -1,3 +1,4 @@
+import functools
 import math
 
 import jax
@@ -65,17 +66,41 @@
 
 
 def main_kernel(
-    state, mask, cot, encw, params, upw, downw, decw, pack, spread,
+    scale, state, mask, cot, encw, bias_in, depth_in, gain_in, upt, downw, dect, pack, spread,
     out, up_out, down_out, depth_out,
     taps, pad_one, side_one, pad_two, side_two, pad_g, side_g, grad, conv, std_one, std_two, inv_one, inv_two,
     act_one, slope_one, normed_one, normed_two, join, grad_mid, depth_acc,
-    upt, downt, dect, enct, own, edge_rows, line_out, line_in, send_sem, recv_sem,
+    upw, downt, decw, enct, own, edge_rows, line_out, line_in, send_sem, recv_sem,
+    tall, params, sums, half_out, half_in, quarter_out, quarter_in, slot_sum, slot_out, slot_in, slot_done, gathered,
+    depth_own, depth_got, depth_mid, depth_peer, depth_all, sum_send, sum_recv,
 ):
     lat, lon = lax.axis_index("lat"), lax.axis_index("lon")
     lats, lons = lax.axis_size("lat"), lax.axis_size("lon")
     has_north, has_south = lat > 0, lat < lats - 1
     north, south = lat - 1, lat + 1
     east, west = lax.rem(lon + 1, lons), lax.rem(lon + lons - 1, lons)
+    x_at, core = lat // 4, lax.rem(lat, 2)
+    member = lon // 2 * 4 + lax.rem(lon, 2) * 2 + lax.rem(lat // 2, 2)
+
+    def core_peer():
+        return (lat + 1 - 2 * core, lon)
+
+    def line_peer(d):
+        return (lax.rem(x_at + d, 4) * 4 + lax.rem(lat, 4), lon)
+
+    def chip_peer(d):
+        flip, step = d // 4, d % 4
+        side = 1 - core if flip else core
+        return (lax.rem(x_at + step, 4) * 4 + lax.rem(lat // 2, 2) * 2 + side, lon)
+
+    def member_at(d):
+        return lax.rem(member + d, 16)
+
+    def plane_peer(d):
+        other = member_at(d)
+        z_at, y_at = other // 4, lax.rem(other, 4)
+        return (x_at * 4 + lax.rem(y_at, 2) * 2 + core, z_at * 2 + y_at // 2)
+
     lat_of = {0: lat, 1: south, -1: north}
     lon_of = {0: lon, 1: east, -1: west}
 
@@ -91,6 +116,9 @@
     for step_lat, step_lon in STEPS:
         when_lat(step_lat, lambda a=step_lat, b=step_lon: pl.semaphore_signal(
             barrier, inc=1, device_id=(lat_of[a], lon_of[b]), device_id_type=MESH))
+
+    for peer in [chip_peer(d) for d in range(1, 8)] + [plane_peer(d) for d in range(1, 16)]:
+        pl.semaphore_signal(barrier, inc=1, device_id=peer, device_id_type=MESH)
 
     def copy_of(turn, m):
         if m == 0:
@@ -143,7 +171,7 @@
             return pltpu.roll(jnp.where(lane < s, edge, main), COLS - s, 2)
         return pltpu.roll(jnp.where(lane >= COLS + s, edge, main), -s, 2)
 
-    def depthwise(pad, side, target, adjoint):
+    def depthwise(pad, side, target, adjoint, first_block=0, last_block=BLOCKS):
         def block(b, carry):
             at = pl.ds(pl.multiple_of(8 * b, 8), 8)
             main, edge = pad[:, at, :], side[:, at, :]
@@ -155,9 +183,9 @@
                     total = total + taps[7 * i + j, at, :][None] * moved[first : first + ROWS]
             target[:, at, :] = total
             return carry
-        lax.fori_loop(0, BLOCKS, block, 0)
-
-    def depth_terms(pad, side, fresh):
+        lax.fori_loop(first_block, last_block, block, 0)
+
+    def depth_terms(pad, side, fresh, first_block=0, last_block=BLOCKS):
         def block(b, carry):
             at = pl.ds(pl.multiple_of(8 * b, 8), 8)
             main, edge, slope = pad[:, at, :], side[:, at, :], grad[:, at, :]
@@ -170,7 +198,7 @@
                     else:
                         depth_acc[7 * i + j, at, :] += term
             return carry
-        lax.fori_loop(0, BLOCKS, block, 0)
+        lax.fori_loop(first_block, last_block, block, 0)
 
     def over_chunks(body):
         lax.fori_loop(0, CHUNKS, lambda k, c: (body(k), c)[1], 0)
@@ -183,6 +211,12 @@
         return jnp.concatenate(
             [ref[pl.ds(2 * k + q, LEVELS, stride=ROWS), :] for q in range(2)], axis=1)
 
+    tall[...] = jnp.zeros_like(tall)
+    for i in range(7):
+        tall[7 * i : 7 * i + 7, :WIDTH] = depth_in[i]
+    tall[49:50, :WIDTH] = bias_in[...]
+    tall[50:51, :WIDTH] = gain_in[...]
+    params[...] = tall[...].T[:WIDTH]
     bias = params[:, 49:50]
     gain = params[:, 50:51]
 
@@ -204,7 +238,7 @@
             for part in (48, 112):
                 line_in[turn, pl.ds(part, 16)] = jnp.zeros((16, SPAN), BF16)
 
-    peers = 2 + 3 * jnp.minimum(lat, 1) + 3 * jnp.minimum(lats - 1 - lat, 1)
+    peers = 24 + 3 * jnp.minimum(lat, 1) + 3 * jnp.minimum(lats - 1 - lat, 1)
     pl.semaphore_wait(barrier, peers)
     send_halo(0)
 
@@ -212,9 +246,10 @@
         ends(turn)
     for t in range(49):
         taps[t] = jnp.broadcast_to(params[:, t : t + 1], (WIDTH, COLS))
-    upt[...] = upw[...].astype(F32).T.astype(BF16)
+    upw[...] = upt[...].astype(F32).T.astype(BF16)
+    sums[...] = jnp.zeros_like(sums)
     downt[...] = downw[...].astype(F32).T.astype(BF16)
-    dect[...] = decw[...].astype(F32).T.astype(BF16)
+    decw[...] = dect[...].astype(F32).T.astype(BF16)
     enct[...] = encw[...].astype(F32).T.astype(BF16)
 
     take_halo(0, pad_one, side_one)
@@ -248,28 +283,17 @@
     take_halo(1, pad_two, side_two)
     depthwise(pad_two, side_two, conv, False)
 
-    def reverse(k, turn, upstream, normed, value, slope, std, inv, fresh):
+    def reverse(k, turn, upstream, normed, value, slope, std, inv):
         ocean = mask_of(k)
         grad_join = dot(dect[...], (ocean * upstream).astype(BF16))
         join[k] = grad_join
         grad_branch = (ocean * grad_join).astype(BF16)
         grad_pre = (dot(downt[...], grad_branch) * slope).astype(BF16)
         grad_norm = dot(upt[...], grad_pre)
-        up_term = dot_nt(grad_pre, normed)
-        down_term = dot_nt(value, grad_branch)
-        if fresh:
-            @pl.when(k == 0)
-            def _():
-                up_out[...] = up_term
-                down_out[...] = down_term
-
-            @pl.when(k > 0)
-            def _():
-                up_out[...] += up_term
-                down_out[...] += down_term
-        else:
-            up_out[...] += up_term
-            down_out[...] += down_term
+        for which, term in ((0, dot_nt(normed, grad_pre)), (1, dot_nt(grad_branch, value))):
+            for part in range(3):
+                sums[which, part, :WIDTH, :] += term[:, SPAN * part : SPAN * (part + 1)]
+            sums[which, 3, :WIDTH, : HIDDEN - 3 * SPAN] += term[:, 3 * SPAN :]
         standard = pair(std, k)
         grad_hat = grad_norm * gain
         first = jnp.sum(grad_hat, axis=0, keepdims=True) * (1.0 / WIDTH)
@@ -281,7 +305,7 @@
     def late(k):
         normed = normalize(k, std_two, inv_two, normed_two)
         value, slope = gelu_parts(dot(upw[...], normed))
-        reverse(k, 2, levels_of(cot, k), normed, value.astype(BF16), slope, std_two, inv_two, True)
+        reverse(k, 2, levels_of(cot, k), normed, value.astype(BF16), slope, std_two, inv_two)
 
     over_chunks(late)
     send_halo(2)
@@ -293,13 +317,117 @@
         grad_input = (join[k] + pair(conv, k)).astype(BF16)
         upstream = levels_of(cot, k) + dot(enct[...], grad_input)
         grad_mid[k] = upstream
-        reverse(k, 3, upstream, normed_one[k], act_one[k], slope_one[k].astype(F32), std_one, inv_one, False)
+        reverse(k, 3, upstream, normed_one[k], act_one[k], slope_one[k].astype(F32), std_one, inv_one)
 
     over_chunks(early)
     send_halo(3)
-    depth_terms(pad_one, side_one, False)
+
+    def remote(src, dst, slot, peer):
+        return pltpu.make_async_remote_copy(
+            src_ref=src, dst_ref=dst, send_sem=sum_send.at[slot], recv_sem=sum_recv.at[slot],
+            device_id=peer, device_id_type=MESH)
+
+    half = remote(half_out, half_in, 0, core_peer())
+    quarters = [
+        remote(quarter_out.at[lax.rem(x_at + d, 4)], quarter_in.at[d - 1], d, line_peer(d)) for d in range(1, 4)]
+
+    def slot_copy(d):
+        other = jnp.minimum(member_at(d), 12)
+        rows = pl.ds(pl.multiple_of(16 * other, 16), 16)
+        return remote(slot_out.at[rows], slot_in.at[d - 1], 3 + d, plane_peer(d))
+
+    def done_copy(d):
+        return remote(slot_done, gathered.at[core, x_at, mine], 18 + d, plane_peer(d))
+
+    def line_copy(d):
+        return remote(gathered.at[core, x_at], gathered.at[core, x_at], 33 + d, line_peer(d))
+
+    back = remote(gathered.at[core], gathered.at[core], 37, core_peer())
+    mine = pl.ds(pl.multiple_of(16 * jnp.minimum(member, 12), 16), 16)
+
+    def depth_copy(d):
+        return remote(depth_own.at[member_at(d)], depth_got.at[d - 1], 37 + d, plane_peer(d))
+
+    def peer_copy(d):
+        return remote(depth_mid, depth_peer.at[d - 1], 52 + d, chip_peer(d))
+
+    def spread_copy(d):
+        return remote(depth_all.at[member], depth_all.at[member], 59 + d, plane_peer(d))
+
+    def owner(index):
+        return lambda run: pl.when(index < 13)(run)
+
+    half_out[...] = sums[1 - core].astype(BF16)
+    half.start()
+    depth_terms(pad_one, side_one, False, 0, 9)
+
+    half.wait_recv()
+    for part in range(4):
+        quarter_out[part] = (sums[core, part] + half_in[part].astype(F32)).astype(BF16)
+    for copy in quarters:
+        copy.start()
+    slot_sum[...] = sums[core, x_at] + half_in[x_at].astype(F32)
+    depth_terms(pad_one, side_one, False, 9, BLOCKS)
+
+    for copy in quarters:
+        copy.wait_recv()
+    slot_sum[...] = slot_sum[...] + (
+        quarter_in[0].astype(F32) + quarter_in[1].astype(F32) + quarter_in[2].astype(F32))
+    slot_out[...] = slot_sum[...].astype(BF16)
+    for d in range(1, 16):
+        owner(member_at(d))(lambda d=d: slot_copy(d).start())
+
+    column = lax.broadcasted_iota(jnp.int32, (WIDTH, COLS), 1)
+    picked = jnp.zeros((WIDTH, COLS), F32)
+    for t in range(49):
+        picked = jnp.where(column == t, jnp.sum(depth_acc[t], axis=1, keepdims=True), picked)
+    turned = jnp.concatenate([picked, jnp.zeros((56, COLS), F32)], axis=0).T
+    for piece in range(16):
+        depth_own[piece] = turned[
+            8 * (piece // 2) : 8 * (piece // 2) + 8, COLS * (piece % 2) : COLS * (piece % 2) + COLS]
+    for d in range(1, 16):
+        depth_copy(d).start()
+
     take_halo(3, pad_g, side_g)
-    depthwise(pad_g, side_g, conv, True)
+    depthwise(pad_g, side_g, conv, True, 0, 8)
+
+    @pl.when(member < 13)
+    def _():
+        total = slot_sum[mine, :]
+        for d in range(1, 16):
+            slot_copy(d).wait_recv()
+            total = total + slot_in[d - 1].astype(F32)
+        total = (total * scale).astype(BF16)
+        slot_done[...] = total
+        gathered[core, x_at, mine, :] = total
+        for d in range(1, 16):
+            done_copy(d).start()
+
+    total = depth_own[member]
+    for d in range(1, 16):
+        depth_copy(d).wait_recv()
+        total = total + depth_got[d - 1]
+    depth_mid[...] = total
+    for d in range(1, 8):
+        peer_copy(d).start()
+    depthwise(pad_g, side_g, conv, True, 8, 16)
+
+    for d in range(1, 16):
+        owner(member_at(16 - d))(lambda d=d: done_copy(d).wait_recv())
+    for d in range(1, 4):
+        line_copy(d).start()
+    total = depth_mid[...]
+    for d in range(1, 8):
+        peer_copy(d).wait_recv()
+        total = total + depth_peer[d - 1]
+    depth_all[member] = total * scale
+    for d in range(1, 16):
+        spread_copy(d).start()
+    depthwise(pad_g, side_g, conv, True, 16, BLOCKS)
+
+    for d in range(1, 4):
+        line_copy(d).wait_recv()
+    back.start()
 
     def last(k):
         grad_input = (join[k] + pair(conv, k)).astype(BF16)
@@ -308,27 +436,50 @@
             out[pl.ds(2 * k + q, LEVELS, stride=ROWS), :] = result[:, COLS * q : COLS * (q + 1)]
 
     over_chunks(last)
-    column = lax.broadcasted_iota(jnp.int32, (WIDTH, COLS), 1)
-    picked = jnp.zeros((WIDTH, COLS), F32)
-    for t in range(49):
-        picked = jnp.where(column == t, jnp.sum(depth_acc[t], axis=1, keepdims=True), picked)
-    depth_out[...] = picked
+    for d in range(1, 16):
+        spread_copy(d).wait_recv()
+    for piece in range(16):
+        row, left = 8 * (piece // 2), COLS * (piece % 2)
+        width = min(COLS, WIDTH - left)
+        for t in range(row, min(row + 8, 49)):
+            depth_out[t // 7, t % 7 : t % 7 + 1, left : left + width] = depth_all[piece, t - row : t - row + 1, :width]
+    back.wait_recv()
+    for which, target in ((0, up_out), (1, down_out)):
+        for part in range(4):
+            left = SPAN * part
+            width = min(SPAN, HIDDEN - left)
+            target[:, left : left + width] = gathered[which, part].astype(F32)[:WIDTH, :width]
+
+    half.wait_send()
+    for copy in quarters:
+        copy.wait_send()
+    back.wait_send()
+    for d in range(1, 4):
+        line_copy(d).wait_send()
+    for d in range(1, 8):
+        peer_copy(d).wait_send()
+    for d in range(1, 16):
+        owner(member_at(d))(lambda d=d: slot_copy(d).wait_send())
+        owner(member)(lambda d=d: done_copy(d).wait_send())
+        depth_copy(d).wait_send()
+        spread_copy(d).wait_send()
     for turn in range(4):
         for m in range(8):
             when_lat(STEPS[m][0], lambda m=m: copy_of(turn, m).wait_send())
 
 
-def main_call(*operands):
+def main_call(scale, *operands):
     vmem = pl.BlockSpec(memory_space=pltpu.VMEM)
     padded = pltpu.VMEM((14, WIDTH, COLS), F32)
     plane = pltpu.VMEM((ROWS, WIDTH, COLS), F32)
+    tile = (8, COLS)
     return pl.pallas_call(
-        main_kernel,
+        functools.partial(main_kernel, scale),
         out_shape=[
             jax.ShapeDtypeStruct((LEVELS * ROWS, COLS), F32),
-            jax.ShapeDtypeStruct((HIDDEN, WIDTH), F32),
-            jax.ShapeDtypeStruct((HIDDEN, WIDTH), F32),
-            jax.ShapeDtypeStruct((WIDTH, COLS), F32),
+            jax.ShapeDtypeStruct((WIDTH, HIDDEN), F32),
+            jax.ShapeDtypeStruct((WIDTH, HIDDEN), F32),
+            jax.ShapeDtypeStruct((7, 7, WIDTH), F32),
         ],
         in_specs=[vmem] * len(operands),
         out_specs=[vmem] * 4,
@@ -345,9 +496,9 @@
             pltpu.VMEM((CHUNKS, WIDTH, SPAN), F32),
             pltpu.VMEM((CHUNKS, LEVELS, SPAN), F32),
             pltpu.VMEM((49, WIDTH, COLS), F32),
-            pltpu.VMEM((WIDTH, HIDDEN), BF16),
             pltpu.VMEM((HIDDEN, WIDTH), BF16),
-            pltpu.VMEM((WIDTH, LEVELS), BF16),
+            pltpu.VMEM((HIDDEN, WIDTH), BF16),
+            pltpu.VMEM((LEVELS, WIDTH), BF16),
             pltpu.VMEM((LEVELS, WIDTH), BF16),
             pltpu.VMEM((4, ROWS, 208, COLS), BF16),
             pltpu.VMEM((4, 2, 3, 208, COLS), BF16),
@@ -355,6 +506,25 @@
             pltpu.VMEM((4, 128, SPAN), BF16),
             pltpu.SemaphoreType.DMA((4, 8)),
             pltpu.SemaphoreType.DMA((4, 8)),
+            pltpu.VMEM((128, SPAN), F32),
+            pltpu.VMEM((WIDTH, COLS), F32),
+            pltpu.VMEM((2, 4, 208, SPAN), F32),
+            pltpu.VMEM((4, 208, SPAN), BF16),
+            pltpu.VMEM((4, 208, SPAN), BF16),
+            pltpu.VMEM((4, 208, SPAN), BF16),
+            pltpu.VMEM((3, 208, SPAN), BF16),
+            pltpu.VMEM((208, SPAN), F32),
+            pltpu.VMEM((208, SPAN), BF16),
+            pltpu.VMEM((15, 16, SPAN), BF16),
+            pltpu.VMEM((16, SPAN), BF16),
+            pltpu.VMEM((2, 4, 208, SPAN), BF16),
+            pltpu.VMEM((16,) + tile, F32),
+            pltpu.VMEM((15,) + tile, F32),
+            pltpu.VMEM(tile, F32),
+            pltpu.VMEM((7,) + tile, F32),
+            pltpu.VMEM((16,) + tile, F32),
+            pltpu.SemaphoreType.DMA((75,)),
+            pltpu.SemaphoreType.DMA((75,)),
         ],
         compiler_params=pltpu.CompilerParams(
             collective_id=0, has_side_effects=True, vmem_limit_bytes=58 * 1024 * 1024),
@@ -365,23 +535,18 @@
     ocean_state, ocean_mask, cotangent, encoder_weight, encoder_bias, depth_weight,
     norm_gain, up_weight, down_weight, decoder_weight,
 ):
-    total_rows = ROWS * lax.axis_size("lat")
-    total_cols = COLS * lax.axis_size("lon")
-    params = jnp.concatenate(
-        [depth_weight.reshape(WIDTH, 49), encoder_bias[:, None], norm_gain[:, None], jnp.zeros((WIDTH, 77), F32)],
-        axis=1)
+    cells = ROWS * lax.axis_size("lat") * COLS * lax.axis_size("lon")
     pack, spread = edge_tables()
     state_grad, up_sum, down_sum, depth_sum = main_call(
+        1.0 / math.sqrt(cells),
         ocean_state.reshape(LEVELS * ROWS, COLS), ocean_mask, cotangent.reshape(LEVELS * ROWS, COLS),
-        encoder_weight, params, up_weight, down_weight, decoder_weight,
-        jnp.asarray(pack), jnp.asarray(spread))
-    joined = jnp.concatenate([up_sum, down_sum, jnp.pad(depth_sum, ((0, 0), (0, WIDTH - COLS)))], axis=0)
-    summed = lax.psum(joined, ("lat", "lon")) * (1.0 / math.sqrt(total_rows * total_cols))
+        encoder_weight, encoder_bias[None, :], jnp.transpose(depth_weight, (1, 2, 0)), norm_gain[None, :],
+        up_weight.T, down_weight, decoder_weight.T, jnp.asarray(pack), jnp.asarray(spread))
     return (
         state_grad.reshape(ocean_state.shape),
-        summed[:HIDDEN],
-        summed[HIDDEN : 2 * HIDDEN].T,
-        summed[2 * HIDDEN :, :49].reshape(WIDTH, 7, 7),
+        up_sum.T,
+        down_sum,
+        jnp.transpose(depth_sum, (2, 0, 1)),
     )
 
 

time: 255 us -> 98.2 us (0.39)
  waiting for transfers between devices: 147 us -> 0 us
  Pallas kernels: 78.4 us -> 92.6 us
  between operations: 14.1 us -> 0.65 us
  other arithmetic: 5.26 us -> 0 us
  local copies, waits for them, and re-layouts: 9.95 us -> 4.7 us
    psum x1 -> x0, waiting for transfers between devices: 147 us -> none  [per_device(): lax.psum(joined, ('lat', 'lon'))]
    pallas_call x1, Pallas kernels: 78.4 us -> 92.6 us  [main_call(): pl.pallas_call(functools.partial(main_kernel, scale), out_shape=[jax.Shap...]
    concatenate x2 -> x0, other arithmetic: 3.59 us -> none  [the longest x1 2.83 us: per_device(): jnp.concatenate([up_sum, down_sum, jnp.pad(depth_sum, ((0, 0), (0, WIDTH...]
    unnamed x7 -> x10, local copies, waits for them, and re-layouts: 6.5 us -> 4.7 us
  transfers between devices with their start and end apart: 1 -> 0, of which waited for: 1 -> 0; matrix products, arithmetic and copies ran while one was open for 0% -> 0% of each run, Pallas kernels for 0% -> 0%
where the time goes in v1:
time: 98.2 us; the launch traced here: 97.9 us
  Pallas kernels  92.6 us (94%)
  local copies, waits for them, and re-layouts  4.7 us (5%)
    pallas_call x1, Pallas kernels, main_call(): pl.pallas_call(functools.partial(main_kernel, scale), out_shape=[jax.Shap...  92.6 us
    unnamed x10, local copies, waits for them, and re-layouts  4.7 us

profile of v1, /device:TPU:1, one launch (start us, length us, event | category | flops | bytes accessed | tf_op | source)
XLA Modules:
  0.0 97.9 jit_solution(10504658500813816300)
XLA Ops:
  0.6 92.6 %shard_map.147 = (f32[800,128]{1,0:T(8,128)}, f32[200,800]{1,0:T(8,128)}, f32[200,800]{1,0:T(8,128)}, f32[7,7,200]{2,1,0:T(8,128)}) custom-call(f32[800,128]{1,0:T(8,128)} %bitcast.12, s32[8,128]{1,0:T(8,128)} %mask.1, f32[800,128]{1,0:T(8,128)} %bitcast.13, bf16[200,100]{1,0:T(8,128)(2,1)} %encw.1, f32[1,200]{1,0:T(1,128)} %bitcast.18, ...), custom_call_target="tpu_custom_call" | custom-call | tf_op jit(solution)/shard_map/pallas_call | solution.py:476
  93.2 0.0 copy-start.1
  93.2 1.8 %copy.20 = f32[100,8,128]{2,1,0:T(8,128)} copy(f32[100,8,128]{2,1,0:T(8,128)} %bitcast.11) | data formatting | bytes 819200
  95.1 0.0 copy-done.1
  95.1 0.0 copy-start
  95.1 0.9 copy.21
  96.0 0.5 copy-done
  96.5 0.0 copy-start.2
  96.5 0.9 copy.22
  97.3 0.0 copy-done.2
  97.3 0.6 copy.23
Async XLA Ops:
  93.2 1.9 %copy-start.1 = (f32[200,800]{1,0:T(8,128)S(1)}, f32[200,800]{1,0:T(8,128)}, u32[]{:S(2)}) copy-start(f32[200,800]{1,0:T(8,128)} %get-tuple-element.9) | copy-start | bytes 1920004
  95.1 1.4 %copy-start = (f32[200,800]{1,0:T(8,128)S(1)}, f32[200,800]{1,0:T(8,128)}, u32[]{:S(2)}) copy-start(f32[200,800]{1,0:T(8,128)} %get-tuple-element.18) | copy-start | bytes 1920004
  96.5 0.9 copy-start.2

commit v2 on v1

--- a/solution.py
+++ b/solution.py
@@ -24,20 +24,28 @@
 SPAN = 256
 BLOCKS = WIDTH // 8
 
-STEPS = ((1, 0), (-1, 0), (0, 1), (0, -1), (1, 1), (1, -1), (-1, 1), (-1, -1))
-LINES = {2: (16, 16, 32), 3: (80, 80, 32), 4: (48, 0, 16), 5: (112, 64, 16), 6: (0, 48, 16), 7: (64, 112, 16)}
+STEPS = ((-1, 0), (1, 0), (1, 0), (-1, 0), (0, 1), (0, -1), (1, 1), (1, -1), (-1, 1), (-1, -1))
+BANDS = ((0, 1, 0, 2), (6, 0, 1, 2), (5, 0, 0, 1), (2, 1, 2, 1))
+LINES = {4: (16, 16, 32), 5: (80, 80, 32), 6: (48, 0, 16), 7: (112, 64, 16), 8: (0, 48, 16), 9: (64, 112, 16)}
+ORDER = (0, 3, 2, 1)
+BAND_OF = {0: 0, 3: 1, 2: 2, 1: 3}
+MEETS = tuple((0, x, k, k - x) for x in range(3) for k in range(x, 3)) + tuple(
+    (1, x, k, 6 + k - x) for x in range(3) for k in range(x + 1))
 
 
 def edge_tables():
     pack = np.zeros((ROWS * COLS, 128), np.float32)
-    spread = np.zeros((128, 14 * COLS), np.float32)
+    spread = np.zeros((CHUNKS, 128, SPAN), np.float32)
     for side in range(2):
-        for first, rows, sent, filled in ((0, 3, 0, 0), (16, 8, 0, 3), (48, 3, 5, 11)):
-            for q in range(3 * rows):
-                row, k = q // 3, q % 3
-                line = 64 * side + first + q
-                pack[COLS * (sent + row) + (k if side else 125 + k), line] = 1.0
-                spread[line, COLS * (filled + row) + (k if side else 125 + k)] = 1.0
+        for k in range(3):
+            column = k if side else 125 + k
+            for first, step, sent, rows in ((0, 4, 0, 3), (16, 8, 0, 8), (48, 4, 5, 3)):
+                for r in range(rows):
+                    pack[COLS * (sent + r) + column, 64 * side + first + step * k + r] = 1.0
+            for y in range(ROWS):
+                column = 125 + k if side else k
+                for part in (0, 48):
+                    spread[y // 2, part + 24 * side + 8 * k + y, COLS * (y % 2) + column] = 1.0
     return pack.astype(jnp.bfloat16), spread.astype(jnp.bfloat16)
 
 
@@ -67,12 +75,13 @@
 
 def main_kernel(
     scale, state, mask, cot, encw, bias_in, depth_in, gain_in, upt, downw, dect, pack, spread,
-    out, up_out, down_out, depth_out,
-    taps, pad_one, side_one, pad_two, side_two, pad_g, side_g, grad, conv, std_one, std_two, inv_one, inv_two,
+    out, gathered, depth_out,
+    taps, pad_one, pad_two, pad_g, grad, conv, std_one, std_two, inv_one, inv_two,
     act_one, slope_one, normed_one, normed_two, join, grad_mid, depth_acc,
     upw, downt, decw, enct, own, edge_rows, line_out, line_in, send_sem, recv_sem,
-    tall, params, sums, half_out, half_in, quarter_out, quarter_in, slot_sum, slot_out, slot_in, slot_done, gathered,
+    tall, params, sums, half_out, half_in, quarter_out, quarter_in, slot_sum, slot_out, slot_in, slot_done,
     depth_own, depth_got, depth_mid, depth_peer, depth_all, sum_send, sum_recv,
+    edges, fix, edge_terms,
 ):
     lat, lon = lax.axis_index("lat"), lax.axis_index("lon")
     lats, lons = lax.axis_size("lat"), lax.axis_size("lon")
@@ -113,7 +122,7 @@
             pl.when(has_north)(run)
 
     barrier = pltpu.get_barrier_semaphore()
-    for step_lat, step_lon in STEPS:
+    for step_lat, step_lon in STEPS[2:]:
         when_lat(step_lat, lambda a=step_lat, b=step_lon: pl.semaphore_signal(
             barrier, inc=1, device_id=(lat_of[a], lon_of[b]), device_id_type=MESH))
 
@@ -121,10 +130,10 @@
         pl.semaphore_signal(barrier, inc=1, device_id=peer, device_id_type=MESH)
 
     def copy_of(turn, m):
-        if m == 0:
-            src, dst = own.at[turn, pl.ds(5, 3)], edge_rows.at[turn, 0]
-        elif m == 1:
-            src, dst = own.at[turn, pl.ds(0, 3)], edge_rows.at[turn, 1]
+        if m < 4:
+            first, side, filled, count = BANDS[m]
+            src = own.at[turn, pl.ds(first, count)]
+            dst = edge_rows.at[turn, side, pl.ds(filled, count)]
         else:
             first, filled, count = LINES[m]
             src, dst = line_out.at[turn, pl.ds(first, count)], line_in.at[turn, pl.ds(filled, count)]
@@ -132,26 +141,52 @@
             src_ref=src, dst_ref=dst, send_sem=send_sem.at[turn, m], recv_sem=recv_sem.at[turn, m],
             device_id=(lat_of[STEPS[m][0]], lon_of[STEPS[m][1]]), device_id_type=MESH)
 
-    def send_halo(turn):
-        for m in (0, 1):
-            when_lat(STEPS[m][0], lambda m=m: copy_of(turn, m).start())
+    def send_lines(turn):
         flat = jnp.concatenate([own[turn, r] for r in range(ROWS)], axis=1)
         picked = dot(flat, pack[...])
         picked = jnp.concatenate([picked, jnp.zeros((48, 128), F32)], axis=0)
         line_out[turn] = picked.T.astype(BF16)
-        for m in range(2, 8):
+        for m in range(4, 10):
             when_lat(STEPS[m][0], lambda m=m: copy_of(turn, m).start())
 
-    def take_halo(turn, pad, side):
-        for m in range(8):
+    def take_rows(turn, pad):
+        for m in range(4):
             when_lat(-STEPS[m][0], lambda m=m: copy_of(turn, m).wait_recv())
         for r in range(3):
             pad[r] = edge_rows[turn, 0, r].astype(F32)[:WIDTH]
             pad[11 + r] = edge_rows[turn, 1, r].astype(F32)[:WIDTH]
-        lines = line_in[turn].astype(F32).T[:WIDTH].astype(BF16)
-        wide = dot(lines, spread[...])
-        for r in range(14):
-            side[r] = wide[:, COLS * r : COLS * (r + 1)]
+
+    def take_lines(turn, slot, adjoint):
+        for m in range(4, 10):
+            when_lat(-STEPS[m][0], lambda m=m: copy_of(turn, m).wait_recv())
+        lines = line_in[turn].astype(F32)
+        for side in range(2):
+            for k in range(3):
+                base, at = 64 * side, 3 * side + k
+                edges[slot, at, 0:3] = lines[base + 4 * k : base + 4 * k + 3]
+                edges[slot, at, 3:11] = lines[base + 16 + 8 * k : base + 24 + 8 * k]
+                edges[slot, at, 11:14] = lines[base + 48 + 4 * k : base + 51 + 4 * k]
+        fixes = [jnp.zeros((8, SPAN), F32)] * 6
+        for i in range(7):
+            for side, x, k, j in MEETS:
+                t = 48 - (7 * i + j) if adjoint else 7 * i + j
+                fixes[3 * side + x] = fixes[3 * side + x] + tall[t : t + 1] * edges[slot, 3 * side + k, i : i + 8]
+        total = jnp.concatenate(fixes, axis=0)
+        coarse = total.astype(BF16).astype(F32)
+        fix[...] = jnp.concatenate([coarse, total - coarse, jnp.zeros((32, SPAN), F32)], axis=0).T[:WIDTH].astype(BF16)
+
+    def edge_depth(turn, slot, fresh):
+        mine = line_out[turn].astype(F32)
+        for i in range(7):
+            for j in (0, 1, 2, 4, 5, 6):
+                term = jnp.zeros((8, SPAN), F32)
+                for side, x, k, at in MEETS:
+                    if at == j:
+                        base = (16 if side else 80) + 8 * x
+                        term = term + mine[base : base + 8] * edges[slot, 3 * side + k, i : i + 8]
+                term = jnp.sum(term, axis=0, keepdims=True)
+                row = pl.ds(7 * i + j, 1)
+                edge_terms[row] = term if fresh else edge_terms[row] + term
 
     def keep(turn, k, value, pad):
         rounded = value.astype(BF16)
@@ -160,37 +195,67 @@
         for q in range(2):
             pad[3 + 2 * k + q] = again[:, COLS * q : COLS * (q + 1)]
             own[turn, 2 * k + q] = filled[:, COLS * q : COLS * (q + 1)]
-        return again
-
-    lane = lax.broadcasted_iota(jnp.int32, (14, 8, COLS), 2)
-
-    def shifted(main, edge, s):
+        m = BAND_OF[k]
+        if turn > 0:
+            when_lat(STEPS[m][0], lambda: copy_of(turn, m).start())
+
+    lane = lax.broadcasted_iota(jnp.int32, (1, 8, COLS), 2)
+
+    def shifted(main, s):
         if s == 0:
             return main
         if s > 0:
-            return pltpu.roll(jnp.where(lane < s, edge, main), COLS - s, 2)
-        return pltpu.roll(jnp.where(lane >= COLS + s, edge, main), -s, 2)
-
-    def depthwise(pad, side, target, adjoint, first_block=0, last_block=BLOCKS):
+            return pltpu.roll(jnp.where(lane < s, 0.0, main), COLS - s, 2)
+        return pltpu.roll(jnp.where(lane >= COLS + s, 0.0, main), -s, 2)
+
+    def tap(i, j, at, adjoint):
+        return taps[48 - (7 * i + j) if adjoint else 7 * i + j, at, :][None]
+
+    def depthwise(pad, target, adjoint, first_block=0, last_block=BLOCKS):
         def block(b, carry):
             at = pl.ds(pl.multiple_of(8 * b, 8), 8)
-            main, edge = pad[:, at, :], side[:, at, :]
-            total = jnp.zeros((ROWS, 8, COLS), F32)
+            main = pad[3:11, at, :]
+            total = None
             for j in range(7):
-                moved = shifted(main, edge, 3 - j if adjoint else j - 3)
-                for i in range(7):
-                    first = 6 - i if adjoint else i
-                    total = total + taps[7 * i + j, at, :][None] * moved[first : first + ROWS]
+                moved = shifted(main, j - 3)
+                for i in (3, 0, 1, 2, 4, 5, 6):
+                    low, high = max(0, 3 - i), min(8, 11 - i)
+                    term = tap(i, j, at, adjoint) * moved[low + i - 3 : high + i - 3]
+                    if total is None:
+                        total = term
+                        continue
+                    pieces = [total[:low]] if low else []
+                    pieces.append(total[low:high] + term)
+                    pieces += [total[high:]] if high < 8 else []
+                    total = jnp.concatenate(pieces, axis=0) if len(pieces) > 1 else pieces[0]
             target[:, at, :] = total
             return carry
         lax.fori_loop(first_block, last_block, block, 0)
 
-    def depth_terms(pad, side, fresh, first_block=0, last_block=BLOCKS):
+    def depthwise_ends(pad, target, adjoint):
         def block(b, carry):
             at = pl.ds(pl.multiple_of(8 * b, 8), 8)
-            main, edge, slope = pad[:, at, :], side[:, at, :], grad[:, at, :]
+            top, bottom = pad[0:3, at, :], pad[11:14, at, :]
+            high, low = [target[y, at, :][None] for y in range(3)], [target[5 + y, at, :][None] for y in range(3)]
             for j in range(7):
-                moved = shifted(main, edge, j - 3)
+                above, below = shifted(top, j - 3), shifted(bottom, j - 3)
+                for i in range(3):
+                    weight, under = tap(i, j, at, adjoint), tap(6 - i, j, at, adjoint)
+                    for y in range(3 - i):
+                        high[y] = high[y] + weight * above[y + i : y + i + 1]
+                        low[2 - y] = low[2 - y] + under * below[2 - y - i : 3 - y - i]
+            for y in range(3):
+                target[y, at, :] = high[y][0]
+                target[5 + y, at, :] = low[y][0]
+            return carry
+        lax.fori_loop(0, BLOCKS, block, 0)
+
+    def depth_terms(pad, fresh, first_block=0, last_block=BLOCKS):
+        def block(b, carry):
+            at = pl.ds(pl.multiple_of(8 * b, 8), 8)
+            main, slope = pad[:, at, :], grad[:, at, :]
+            for j in range(7):
+                moved = shifted(main, j - 3)
                 for i in range(7):
                     term = jnp.sum(slope * moved[i : i + ROWS], axis=0)
                     if fresh:
@@ -200,8 +265,12 @@
             return carry
         lax.fori_loop(first_block, last_block, block, 0)
 
+    def whole(k):
+        return pair(conv, k) + dot(fix[...], spread[k])
+
     def over_chunks(body):
-        lax.fori_loop(0, CHUNKS, lambda k, c: (body(k), c)[1], 0)
+        for k in ORDER:
+            body(k)
 
     def mask_of(k):
         both = jnp.concatenate([mask[pl.ds(2 * k, 1), :], mask[pl.ds(2 * k + 1, 1), :]], axis=1)
@@ -240,7 +309,9 @@
 
     peers = 24 + 3 * jnp.minimum(lat, 1) + 3 * jnp.minimum(lats - 1 - lat, 1)
     pl.semaphore_wait(barrier, peers)
-    send_halo(0)
+    for m in range(4):
+        when_lat(STEPS[m][0], lambda m=m: copy_of(0, m).start())
+    send_lines(0)
 
     for turn in range(4):
         ends(turn)
@@ -248,15 +319,18 @@
         taps[t] = jnp.broadcast_to(params[:, t : t + 1], (WIDTH, COLS))
     upw[...] = upt[...].astype(F32).T.astype(BF16)
     sums[...] = jnp.zeros_like(sums)
+    edge_terms[...] = jnp.zeros_like(edge_terms)
     downt[...] = downw[...].astype(F32).T.astype(BF16)
     decw[...] = dect[...].astype(F32).T.astype(BF16)
     enct[...] = encw[...].astype(F32).T.astype(BF16)
 
-    take_halo(0, pad_one, side_one)
-    depthwise(pad_one, side_one, conv, False)
+    depthwise(pad_one, conv, False)
+    take_rows(0, pad_one)
+    depthwise_ends(pad_one, conv, False)
+    take_lines(0, 0, False)
 
     def normalize(k, std, inv, normed):
-        value = pair(conv, k)
+        value = whole(k)
         centre = value - jnp.sum(value, axis=0, keepdims=True) * (1.0 / WIDTH)
         inverse = lax.rsqrt(jnp.sum(centre * centre, axis=0, keepdims=True) * (1.0 / WIDTH) + EPSILON)
         standard = centre * inverse
@@ -279,9 +353,11 @@
         encode(k, middle, 1, pad_two)
 
     over_chunks(forward)
-    send_halo(1)
-    take_halo(1, pad_two, side_two)
-    depthwise(pad_two, side_two, conv, False)
+    send_lines(1)
+    depthwise(pad_two, conv, False)
+    take_rows(1, pad_two)
+    depthwise_ends(pad_two, conv, False)
+    take_lines(1, 1, False)
 
     def reverse(k, turn, upstream, normed, value, slope, std, inv):
         ocean = mask_of(k)
@@ -290,10 +366,6 @@
         grad_branch = (ocean * grad_join).astype(BF16)
         grad_pre = (dot(downt[...], grad_branch) * slope).astype(BF16)
         grad_norm = dot(upt[...], grad_pre)
-        for which, term in ((0, dot_nt(normed, grad_pre)), (1, dot_nt(grad_branch, value))):
-            for part in range(3):
-                sums[which, part, :WIDTH, :] += term[:, SPAN * part : SPAN * (part + 1)]
-            sums[which, 3, :WIDTH, : HIDDEN - 3 * SPAN] += term[:, 3 * SPAN :]
         standard = pair(std, k)
         grad_hat = grad_norm * gain
         first = jnp.sum(grad_hat, axis=0, keepdims=True) * (1.0 / WIDTH)
@@ -301,6 +373,10 @@
         result = inv[k][0:1] * (grad_hat - first - standard * second)
         grad[2 * k], grad[2 * k + 1] = rows_of(result)
         keep(turn, k, result, pad_g)
+        for which, term in ((0, dot_nt(normed, grad_pre)), (1, dot_nt(grad_branch, value))):
+            for part in range(3):
+                sums[which, part, :WIDTH, :] += term[:, SPAN * part : SPAN * (part + 1)]
+            sums[which, 3, :WIDTH, : HIDDEN - 3 * SPAN] += term[:, 3 * SPAN :]
 
     def late(k):
         normed = normalize(k, std_two, inv_two, normed_two)
@@ -308,28 +384,35 @@
         reverse(k, 2, levels_of(cot, k), normed, value.astype(BF16), slope, std_two, inv_two)
 
     over_chunks(late)
-    send_halo(2)
-    depth_terms(pad_two, side_two, True)
-    take_halo(2, pad_g, side_g)
-    depthwise(pad_g, side_g, conv, True)
+    send_lines(2)
+    depth_terms(pad_two, True)
+    edge_depth(2, 1, True)
+    depthwise(pad_g, conv, True)
+    take_rows(2, pad_g)
+    depthwise_ends(pad_g, conv, True)
+    take_lines(2, 2, True)
 
     def early(k):
-        grad_input = (join[k] + pair(conv, k)).astype(BF16)
+        grad_input = (join[k] + whole(k)).astype(BF16)
         upstream = levels_of(cot, k) + dot(enct[...], grad_input)
         grad_mid[k] = upstream
         reverse(k, 3, upstream, normed_one[k], act_one[k], slope_one[k].astype(F32), std_one, inv_one)
 
     over_chunks(early)
-    send_halo(3)
+    send_lines(3)
 
     def remote(src, dst, slot, peer):
         return pltpu.make_async_remote_copy(
             src_ref=src, dst_ref=dst, send_sem=sum_send.at[slot], recv_sem=sum_recv.at[slot],
             device_id=peer, device_id_type=MESH)
 
-    half = remote(half_out, half_in, 0, core_peer())
-    quarters = [
-        remote(quarter_out.at[lax.rem(x_at + d, 4)], quarter_in.at[d - 1], d, line_peer(d)) for d in range(1, 4)]
+    def line_at(d):
+        return lax.rem(x_at + d, 4)
+
+    mine = pl.ds(pl.multiple_of(16 * jnp.minimum(member, 12), 16), 16)
+    halves = [remote(half_out.at[line_at(d)], half_in.at[line_at(d)], 75 + d, core_peer()) for d in range(4)]
+    backs = [remote(gathered.at[core, line_at(d)], gathered.at[core, line_at(d)], 79 + d, core_peer()) for d in range(4)]
+    quarters = [remote(quarter_out.at[line_at(d)], quarter_in.at[d - 1], d, line_peer(d)) for d in range(1, 4)]
 
     def slot_copy(d):
         other = jnp.minimum(member_at(d), 12)
@@ -342,9 +425,6 @@
     def line_copy(d):
         return remote(gathered.at[core, x_at], gathered.at[core, x_at], 33 + d, line_peer(d))
 
-    back = remote(gathered.at[core], gathered.at[core], 37, core_peer())
-    mine = pl.ds(pl.multiple_of(16 * jnp.minimum(member, 12), 16), 16)
-
     def depth_copy(d):
         return remote(depth_own.at[member_at(d)], depth_got.at[d - 1], 37 + d, plane_peer(d))
 
@@ -357,17 +437,18 @@
     def owner(index):
         return lambda run: pl.when(index < 13)(run)
 
-    half_out[...] = sums[1 - core].astype(BF16)
-    half.start()
-    depth_terms(pad_one, side_one, False, 0, 9)
-
-    half.wait_recv()
-    for part in range(4):
-        quarter_out[part] = (sums[core, part] + half_in[part].astype(F32)).astype(BF16)
-    for copy in quarters:
-        copy.start()
+    for d in (1, 2, 3, 0):
+        half_out[line_at(d)] = sums[1 - core, line_at(d)].astype(BF16)
+        halves[d].start()
+    depth_terms(pad_one, False, 0, 6)
+
+    for d in (1, 2, 3):
+        halves[d].wait_recv()
+        quarter_out[line_at(d)] = (sums[core, line_at(d)] + half_in[line_at(d)].astype(F32)).astype(BF16)
+        quarters[d - 1].start()
+    halves[0].wait_recv()
     slot_sum[...] = sums[core, x_at] + half_in[x_at].astype(F32)
-    depth_terms(pad_one, side_one, False, 9, BLOCKS)
+    depth_terms(pad_one, False, 6, BLOCKS)
 
     for copy in quarters:
         copy.wait_recv()
@@ -377,19 +458,18 @@
     for d in range(1, 16):
         owner(member_at(d))(lambda d=d: slot_copy(d).start())
 
+    edge_depth(3, 0, False)
     column = lax.broadcasted_iota(jnp.int32, (WIDTH, COLS), 1)
     picked = jnp.zeros((WIDTH, COLS), F32)
     for t in range(49):
         picked = jnp.where(column == t, jnp.sum(depth_acc[t], axis=1, keepdims=True), picked)
-    turned = jnp.concatenate([picked, jnp.zeros((56, COLS), F32)], axis=0).T
+    turned = jnp.concatenate([picked, jnp.zeros((56, COLS), F32)], axis=0).T[:64] + edge_terms[...]
     for piece in range(16):
         depth_own[piece] = turned[
             8 * (piece // 2) : 8 * (piece // 2) + 8, COLS * (piece % 2) : COLS * (piece % 2) + COLS]
     for d in range(1, 16):
         depth_copy(d).start()
-
-    take_halo(3, pad_g, side_g)
-    depthwise(pad_g, side_g, conv, True, 0, 8)
+    depthwise(pad_g, conv, True, 0, 10)
 
     @pl.when(member < 13)
     def _():
@@ -410,12 +490,13 @@
     depth_mid[...] = total
     for d in range(1, 8):
         peer_copy(d).start()
-    depthwise(pad_g, side_g, conv, True, 8, 16)
+    depthwise(pad_g, conv, True, 10, BLOCKS)
 
     for d in range(1, 16):
         owner(member_at(16 - d))(lambda d=d: done_copy(d).wait_recv())
     for d in range(1, 4):
         line_copy(d).start()
+    backs[0].start()
     total = depth_mid[...]
     for d in range(1, 8):
         peer_copy(d).wait_recv()
@@ -423,19 +504,20 @@
     depth_all[member] = total * scale
     for d in range(1, 16):
         spread_copy(d).start()
-    depthwise(pad_g, side_g, conv, True, 16, BLOCKS)
-
-    for d in range(1, 4):
-        line_copy(d).wait_recv()
-    back.start()
+    take_rows(3, pad_g)
+    depthwise_ends(pad_g, conv, True)
+    take_lines(3, 2, True)
 
     def last(k):
-        grad_input = (join[k] + pair(conv, k)).astype(BF16)
+        grad_input = (join[k] + whole(k)).astype(BF16)
         result = grad_mid[k] + dot(enct[...], grad_input)
         for q in range(2):
             out[pl.ds(2 * k + q, LEVELS, stride=ROWS), :] = result[:, COLS * q : COLS * (q + 1)]
 
     over_chunks(last)
+    for d in (1, 2, 3):
+        line_copy(d).wait_recv()
+        backs[4 - d].start()
     for d in range(1, 16):
         spread_copy(d).wait_recv()
     for piece in range(16):
@@ -443,17 +525,11 @@
         width = min(COLS, WIDTH - left)
         for t in range(row, min(row + 8, 49)):
             depth_out[t // 7, t % 7 : t % 7 + 1, left : left + width] = depth_all[piece, t - row : t - row + 1, :width]
-    back.wait_recv()
-    for which, target in ((0, up_out), (1, down_out)):
-        for part in range(4):
-            left = SPAN * part
-            width = min(SPAN, HIDDEN - left)
-            target[:, left : left + width] = gathered[which, part].astype(F32)[:WIDTH, :width]
-
-    half.wait_send()
-    for copy in quarters:
+    for copy in backs:
+        copy.wait_recv()
+
+    for copy in halves + quarters + backs:
         copy.wait_send()
-    back.wait_send()
     for d in range(1, 4):
         line_copy(d).wait_send()
     for d in range(1, 8):
@@ -464,7 +540,7 @@
         depth_copy(d).wait_send()
         spread_copy(d).wait_send()
     for turn in range(4):
-        for m in range(8):
+        for m in range(10):
             when_lat(STEPS[m][0], lambda m=m: copy_of(turn, m).wait_send())
 
 
@@ -477,15 +553,14 @@
         functools.partial(main_kernel, scale),
         out_shape=[
             jax.ShapeDtypeStruct((LEVELS * ROWS, COLS), F32),
-            jax.ShapeDtypeStruct((WIDTH, HIDDEN), F32),
-            jax.ShapeDtypeStruct((WIDTH, HIDDEN), F32),
+            jax.ShapeDtypeStruct((2, 4, 208, SPAN), BF16),
             jax.ShapeDtypeStruct((7, 7, WIDTH), F32),
         ],
         in_specs=[vmem] * len(operands),
-        out_specs=[vmem] * 4,
+        out_specs=[vmem] * 3,
         scratch_shapes=[
             pltpu.VMEM((49, WIDTH, COLS), F32),
-            padded, padded, padded, padded, padded, padded,
+            padded, padded, padded,
             plane, plane, plane, plane,
             pltpu.VMEM((CHUNKS, 8, SPAN), F32),
             pltpu.VMEM((CHUNKS, 8, SPAN), F32),
@@ -504,8 +579,8 @@
             pltpu.VMEM((4, 2, 3, 208, COLS), BF16),
             pltpu.VMEM((4, 128, SPAN), BF16),
             pltpu.VMEM((4, 128, SPAN), BF16),
-            pltpu.SemaphoreType.DMA((4, 8)),
-            pltpu.SemaphoreType.DMA((4, 8)),
+            pltpu.SemaphoreType.DMA((4, 10)),
+            pltpu.SemaphoreType.DMA((4, 10)),
             pltpu.VMEM((128, SPAN), F32),
             pltpu.VMEM((WIDTH, COLS), F32),
             pltpu.VMEM((2, 4, 208, SPAN), F32),
@@ -517,17 +592,44 @@
             pltpu.VMEM((208, SPAN), BF16),
             pltpu.VMEM((15, 16, SPAN), BF16),
             pltpu.VMEM((16, SPAN), BF16),
-            pltpu.VMEM((2, 4, 208, SPAN), BF16),
             pltpu.VMEM((16,) + tile, F32),
             pltpu.VMEM((15,) + tile, F32),
             pltpu.VMEM(tile, F32),
             pltpu.VMEM((7,) + tile, F32),
             pltpu.VMEM((16,) + tile, F32),
-            pltpu.SemaphoreType.DMA((75,)),
-            pltpu.SemaphoreType.DMA((75,)),
+            pltpu.SemaphoreType.DMA((83,)),
+            pltpu.SemaphoreType.DMA((83,)),
+            pltpu.VMEM((3, 6, 16, SPAN), F32),
+            pltpu.VMEM((WIDTH, COLS), BF16),
+            pltpu.VMEM((64, SPAN), F32),
         ],
         compiler_params=pltpu.CompilerParams(
             collective_id=0, has_side_effects=True, vmem_limit_bytes=58 * 1024 * 1024),
+    )(*operands)
+
+
+def result_kernel(state, gathered, depth, state_out, up_out, down_out, depth_out):
+    state_out[...] = state[...]
+    depth_out[...] = depth[...]
+    for which, target in ((0, up_out), (1, down_out)):
+        for part in range(4):
+            left = SPAN * part
+            width = min(SPAN, HIDDEN - left)
+            target[:, left : left + width] = gathered[which, part].astype(F32)[:WIDTH, :width]
+
+
+def result_call(*operands):
+    vmem = pl.BlockSpec(memory_space=pltpu.VMEM)
+    return pl.pallas_call(
+        result_kernel,
+        out_shape=[
+            jax.ShapeDtypeStruct((LEVELS * ROWS, COLS), F32),
+            jax.ShapeDtypeStruct((WIDTH, HIDDEN), F32),
+            jax.ShapeDtypeStruct((WIDTH, HIDDEN), F32),
+            jax.ShapeDtypeStruct((7, 7, WIDTH), F32),
+        ],
+        in_specs=[vmem] * 3,
+        out_specs=[vmem] * 4,
     )(*operands)
 
 
@@ -537,11 +639,12 @@
 ):
     cells = ROWS * lax.axis_size("lat") * COLS * lax.axis_size("lon")
     pack, spread = edge_tables()
-    state_grad, up_sum, down_sum, depth_sum = main_call(
+    parts = main_call(
         1.0 / math.sqrt(cells),
         ocean_state.reshape(LEVELS * ROWS, COLS), ocean_mask, cotangent.reshape(LEVELS * ROWS, COLS),
         encoder_weight, encoder_bias[None, :], jnp.transpose(depth_weight, (1, 2, 0)), norm_gain[None, :],
         up_weight.T, down_weight, decoder_weight.T, jnp.asarray(pack), jnp.asarray(spread))
+    state_grad, up_sum, down_sum, depth_sum = result_call(*parts)
     return (
         state_grad.reshape(ocean_state.shape),
         up_sum.T,

time: 98.2 us -> 85.2 us (0.87)
  Pallas kernels: 92.6 us -> 84.4 us
  local copies, waits for them, and re-layouts: 4.7 us -> 0 us
    pallas_call x1, Pallas kernels: 92.6 us -> 81.9 us  [main_call(): pl.pallas_call(functools.partial(main_kernel, scale), out_shape=[jax.Shap...]
    unnamed x10 -> x0, local copies, waits for them, and re-layouts: 4.7 us -> none
    pallas_call x0 -> x1, Pallas kernels: none -> 2.57 us  [result_call(): pl.pallas_call(result_kernel, out_shape=[jax.ShapeDtypeStruct((LEVELS * R...]
where the time goes in v2:
time: 85.2 us; the launch traced here: 85.1 us
  Pallas kernels  84.4 us (99%)
    pallas_call x1, Pallas kernels, main_call(): pl.pallas_call(functools.partial(main_kernel, scale), out_shape=[jax.Shap...  81.9 us
    pallas_call x1, Pallas kernels, result_call(): pl.pallas_call(result_kernel, out_shape=[jax.ShapeDtypeStruct((LEVELS * R...  2.57 us

profile of v2, /device:TPU:1, one launch (start us, length us, event | category | flops | bytes accessed | tf_op | source)
XLA Modules:
  0.0 85.1 jit_solution(12227353595833407244)
XLA Ops:
  0.6 81.9 %shard_map.147 = (f32[800,128]{1,0:T(8,128)}, bf16[2,4,208,256]{3,2,1,0:T(8,128)(2,1)}, f32[7,7,200]{2,1,0:T(8,128)}) custom-call(f32[800,128]{1,0:T(8,128)} %bitcast.10, s32[8,128]{1,0:T(8,128)} %mask.1, f32[800,128]{1,0:T(8,128)} %bitcast.11, bf16[200,100]{1,0:T(8,128)(2,1)} %encw.1, f32[1,200]{1,0:T(1,128)} %bitcast.15, f32[7,7,200]{2,1,0:T(8,128)} %bitcast.13, ...), custom_call_target="tpu_custom_call" | custom-call | tf_op jit(solution)/shard_map/pallas_call | solution.py:552
  82.5 2.6 %shard_map.148 = (f32[800,128]{1,0:T(8,128)}, f32[200,800]{1,0:T(8,128)}, f32[200,800]{1,0:T(8,128)}, f32[7,7,200]{2,1,0:T(8,128)}) custom-call(f32[800,128]{1,0:T(8,128)} %get-tuple-element.11.state, bf16[2,4,208,256]{3,2,1,0:T(8,128)(2,1)} %get-tuple-element.12.gathered, f32[7,7,200]{2,1,0:T(8,128)} %get-tuple-element.13.depth), custom_call_target="tpu_custom_call" | custom-call | tf_op jit(solution)/shard_map/pallas_call | solution.py:623

commit v3 on v2

--- a/solution.py
+++ b/solution.py
@@ -22,7 +22,8 @@
 COLS = 128
 CHUNKS = 4
 SPAN = 256
-BLOCKS = WIDTH // 8
+FULL = 208
+BLOCKS = FULL // 16
 
 STEPS = ((-1, 0), (1, 0), (1, 0), (-1, 0), (0, 1), (0, -1), (1, 1), (1, -1), (-1, 1), (-1, -1))
 BANDS = ((0, 1, 0, 2), (6, 0, 1, 2), (5, 0, 0, 1), (2, 1, 2, 1))
@@ -73,16 +74,37 @@
     return jnp.concatenate([ref[2 * k], ref[2 * k + 1]], axis=1)
 
 
+INPUTS = 12
+FIRST = (0, 1, 3, 4, 5, 6)
+
+
+def staged_kernel(scale, *refs):
+    raw, rest, buffers, sems = refs[:INPUTS], refs[INPUTS : -INPUTS - 1], refs[-INPUTS - 1 : -1], refs[-1]
+    copies = [pltpu.make_async_copy(raw[n], buffers[n], sems.at[n]) for n in range(INPUTS)]
+
+    def start():
+        for n in FIRST + tuple(n for n in range(INPUTS) if n not in FIRST):
+            copies[n].start()
+
+    def arrive(first):
+        for n in range(INPUTS):
+            if (n in FIRST) == first:
+                copies[n].wait()
+
+    main_kernel(scale, start, arrive, *buffers, *rest)
+
+
 def main_kernel(
-    scale, state, mask, cot, encw, bias_in, depth_in, gain_in, upt, downw, dect, pack, spread,
+    scale, start, arrive, state, mask, cot, encw, bias_in, depth_in, gain_in, upt, downw, dect, pack, spread,
     out, gathered, depth_out,
-    taps, pad_one, pad_two, pad_g, grad, conv, std_one, std_two, inv_one, inv_two,
+    taps, conv, std_one, std_two, inv_one, inv_two,
     act_one, slope_one, normed_one, normed_two, join, grad_mid, depth_acc,
     upw, downt, decw, enct, own, edge_rows, line_out, line_in, send_sem, recv_sem,
     tall, params, sums, half_out, half_in, quarter_out, quarter_in, slot_sum, slot_out, slot_in, slot_done,
     depth_own, depth_got, depth_mid, depth_peer, depth_all, sum_send, sum_recv,
     edges, fix, edge_terms,
 ):
+    start()
     lat, lon = lax.axis_index("lat"), lax.axis_index("lon")
     lats, lons = lax.axis_size("lat"), lax.axis_size("lon")
     has_north, has_south = lat > 0, lat < lats - 1
@@ -149,12 +171,9 @@
         for m in range(4, 10):
             when_lat(STEPS[m][0], lambda m=m: copy_of(turn, m).start())
 
-    def take_rows(turn, pad):
+    def take_rows(turn):
         for m in range(4):
             when_lat(-STEPS[m][0], lambda m=m: copy_of(turn, m).wait_recv())
-        for r in range(3):
-            pad[r] = edge_rows[turn, 0, r].astype(F32)[:WIDTH]
-            pad[11 + r] = edge_rows[turn, 1, r].astype(F32)[:WIDTH]
 
     def take_lines(turn, slot, adjoint):
         for m in range(4, 10):
@@ -188,85 +207,95 @@
                 row = pl.ds(7 * i + j, 1)
                 edge_terms[row] = term if fresh else edge_terms[row] + term
 
-    def keep(turn, k, value, pad):
-        rounded = value.astype(BF16)
-        again = rounded.astype(F32)
+    def keep(turn, k, value):
         filled = jnp.concatenate([value, jnp.zeros((8, SPAN), F32)], axis=0).astype(BF16)
-        for q in range(2):
-            pad[3 + 2 * k + q] = again[:, COLS * q : COLS * (q + 1)]
-            own[turn, 2 * k + q] = filled[:, COLS * q : COLS * (q + 1)]
+        own[turn, 2 * k], own[turn, 2 * k + 1] = rows_of(filled)
         m = BAND_OF[k]
         if turn > 0:
             when_lat(STEPS[m][0], lambda: copy_of(turn, m).start())
 
-    lane = lax.broadcasted_iota(jnp.int32, (1, 8, COLS), 2)
+    lane = lax.broadcasted_iota(jnp.int32, (1, 16, COLS), 2)
+    nothing = jnp.zeros((), BF16)
 
     def shifted(main, s):
         if s == 0:
             return main
         if s > 0:
-            return pltpu.roll(jnp.where(lane < s, 0.0, main), COLS - s, 2)
-        return pltpu.roll(jnp.where(lane >= COLS + s, 0.0, main), -s, 2)
+            return pltpu.roll(jnp.where(lane < s, nothing, main), COLS - s, 2)
+        return pltpu.roll(jnp.where(lane >= COLS + s, nothing, main), -s, 2)
 
     def tap(i, j, at, adjoint):
         return taps[48 - (7 * i + j) if adjoint else 7 * i + j, at, :][None]
 
-    def depthwise(pad, target, adjoint, first_block=0, last_block=BLOCKS):
+    def over_blocks(body, first_block, last_block):
         def block(b, carry):
-            at = pl.ds(pl.multiple_of(8 * b, 8), 8)
-            main = pad[3:11, at, :]
+            body(pl.ds(pl.multiple_of(16 * b, 16), 16))
+            return carry
+        lax.fori_loop(first_block, last_block, block, 0, unroll=3 if last_block - first_block > 4 else 1)
+
+    def depthwise(turn, adjoint, first_block=0, last_block=BLOCKS):
+        def block(at):
+            main = own[turn, :, at, :]
             total = None
             for j in range(7):
                 moved = shifted(main, j - 3)
+                part = None
                 for i in (3, 0, 1, 2, 4, 5, 6):
                     low, high = max(0, 3 - i), min(8, 11 - i)
                     term = tap(i, j, at, adjoint) * moved[low + i - 3 : high + i - 3]
-                    if total is None:
-                        total = term
+                    if part is None:
+                        part = term
                         continue
-                    pieces = [total[:low]] if low else []
-                    pieces.append(total[low:high] + term)
-                    pieces += [total[high:]] if high < 8 else []
-                    total = jnp.concatenate(pieces, axis=0) if len(pieces) > 1 else pieces[0]
-            target[:, at, :] = total
-            return carry
-        lax.fori_loop(first_block, last_block, block, 0)
-
-    def depthwise_ends(pad, target, adjoint):
-        def block(b, carry):
-            at = pl.ds(pl.multiple_of(8 * b, 8), 8)
-            top, bottom = pad[0:3, at, :], pad[11:14, at, :]
-            high, low = [target[y, at, :][None] for y in range(3)], [target[5 + y, at, :][None] for y in range(3)]
+                    pieces = [part[:low]] if low else []
+                    pieces.append(part[low:high] + term)
+                    pieces += [part[high:]] if high < 8 else []
+                    part = jnp.concatenate(pieces, axis=0)
+                part = part.astype(F32)
+                total = part if total is None else total + part
+            conv[:, at, :] = total
+        over_blocks(block, first_block, last_block)
+
+    def depthwise_ends(turn, adjoint):
+        def block(at):
+            top, bottom = edge_rows[turn, 0, :, at, :], edge_rows[turn, 1, :, at, :]
+            high, low = conv[0:3, at, :], conv[5:8, at, :]
             for j in range(7):
                 above, below = shifted(top, j - 3), shifted(bottom, j - 3)
+                over, under = [None] * 3, [None] * 3
                 for i in range(3):
-                    weight, under = tap(i, j, at, adjoint), tap(6 - i, j, at, adjoint)
+                    weight, mirror = tap(i, j, at, adjoint), tap(6 - i, j, at, adjoint)
                     for y in range(3 - i):
-                        high[y] = high[y] + weight * above[y + i : y + i + 1]
-                        low[2 - y] = low[2 - y] + under * below[2 - y - i : 3 - y - i]
-            for y in range(3):
-                target[y, at, :] = high[y][0]
-                target[5 + y, at, :] = low[y][0]
-            return carry
-        lax.fori_loop(0, BLOCKS, block, 0)
-
-    def depth_terms(pad, fresh, first_block=0, last_block=BLOCKS):
-        def block(b, carry):
-            at = pl.ds(pl.multiple_of(8 * b, 8), 8)
-            main, slope = pad[:, at, :], grad[:, at, :]
+                        term = weight * above[y + i : y + i + 1]
+                        over[y] = term if over[y] is None else over[y] + term
+                        term = mirror * below[2 - y - i : 3 - y - i]
+                        under[2 - y] = term if under[2 - y] is None else under[2 - y] + term
+                high = high + jnp.concatenate(over, axis=0).astype(F32)
+                low = low + jnp.concatenate(under, axis=0).astype(F32)
+            conv[0:3, at, :] = high
+            conv[5:8, at, :] = low
+        over_blocks(block, 0, BLOCKS)
+
+    def depth_terms(turn, upper, fresh, first_block=0, last_block=BLOCKS):
+        def block(at):
+            main = jnp.concatenate(
+                [edge_rows[turn, 0, :, at, :], own[turn, :, at, :], edge_rows[turn, 1, :, at, :]], axis=0)
+            slope = own[upper, :, at, :]
             for j in range(7):
                 moved = shifted(main, j - 3)
                 for i in range(7):
-                    term = jnp.sum(slope * moved[i : i + ROWS], axis=0)
+                    product = slope * moved[i : i + ROWS]
+                    term = product[0]
+                    for y in range(1, ROWS):
+                        term = term + product[y]
+                    term = term.astype(F32)
                     if fresh:
                         depth_acc[7 * i + j, at, :] = term
                     else:
                         depth_acc[7 * i + j, at, :] += term
-            return carry
-        lax.fori_loop(first_block, last_block, block, 0)
+        over_blocks(block, first_block, last_block)
 
     def whole(k):
-        return pair(conv, k) + dot(fix[...], spread[k])
+        return pair(conv, k)[:WIDTH] + dot(fix[...], spread[k])
 
     def over_chunks(body):
         for k in ORDER:
@@ -280,19 +309,20 @@
         return jnp.concatenate(
             [ref[pl.ds(2 * k + q, LEVELS, stride=ROWS), :] for q in range(2)], axis=1)
 
+    arrive(True)
     tall[...] = jnp.zeros_like(tall)
     for i in range(7):
         tall[7 * i : 7 * i + 7, :WIDTH] = depth_in[i]
     tall[49:50, :WIDTH] = bias_in[...]
     tall[50:51, :WIDTH] = gain_in[...]
-    params[...] = tall[...].T[:WIDTH]
-    bias = params[:, 49:50]
-    gain = params[:, 50:51]
-
-    def encode(k, value, turn, pad):
-        keep(turn, k, dot(encw[...], value.astype(BF16)) + bias, pad)
-
-    over_chunks(lambda k: encode(k, levels_of(state, k), 0, pad_one))
+    params[...] = tall[...].T[:FULL]
+    bias = params[:WIDTH, 49:50]
+    gain = params[:WIDTH, 50:51]
+
+    def encode(k, value, turn):
+        keep(turn, k, dot(encw[...], value.astype(BF16)) + bias)
+
+    over_chunks(lambda k: encode(k, levels_of(state, k), 0))
 
     def ends(turn):
         @pl.when(jnp.logical_not(has_north))
@@ -307,6 +337,7 @@
             for part in (48, 112):
                 line_in[turn, pl.ds(part, 16)] = jnp.zeros((16, SPAN), BF16)
 
+    arrive(False)
     peers = 24 + 3 * jnp.minimum(lat, 1) + 3 * jnp.minimum(lats - 1 - lat, 1)
     pl.semaphore_wait(barrier, peers)
     for m in range(4):
@@ -316,7 +347,7 @@
     for turn in range(4):
         ends(turn)
     for t in range(49):
-        taps[t] = jnp.broadcast_to(params[:, t : t + 1], (WIDTH, COLS))
+        taps[t] = jnp.broadcast_to(params[:, t : t + 1], (FULL, COLS)).astype(BF16)
     upw[...] = upt[...].astype(F32).T.astype(BF16)
     sums[...] = jnp.zeros_like(sums)
     edge_terms[...] = jnp.zeros_like(edge_terms)
@@ -324,9 +355,9 @@
     decw[...] = dect[...].astype(F32).T.astype(BF16)
     enct[...] = encw[...].astype(F32).T.astype(BF16)
 
-    depthwise(pad_one, conv, False)
-    take_rows(0, pad_one)
-    depthwise_ends(pad_one, conv, False)
+    depthwise(0, False)
+    take_rows(0)
+    depthwise_ends(0, False)
     take_lines(0, 0, False)
 
     def normalize(k, std, inv, normed):
@@ -347,16 +378,16 @@
         value = value.astype(BF16)
         act_one[k] = value
         slope_one[k] = slope.astype(BF16)
-        features = jnp.concatenate([pad_one[3 + 2 * k], pad_one[4 + 2 * k]], axis=1)
+        features = pair(own.at[0], k).astype(F32)[:WIDTH]
         joined = (features + ocean * dot(downw[...], value)).astype(BF16)
         middle = levels_of(state, k) + ocean * dot(decw[...], joined)
-        encode(k, middle, 1, pad_two)
+        encode(k, middle, 1)
 
     over_chunks(forward)
     send_lines(1)
-    depthwise(pad_two, conv, False)
-    take_rows(1, pad_two)
-    depthwise_ends(pad_two, conv, False)
+    depthwise(1, False)
+    take_rows(1)
+    depthwise_ends(1, False)
     take_lines(1, 1, False)
 
     def reverse(k, turn, upstream, normed, value, slope, std, inv):
@@ -371,8 +402,7 @@
         first = jnp.sum(grad_hat, axis=0, keepdims=True) * (1.0 / WIDTH)
         second = jnp.sum(grad_hat * standard, axis=0, keepdims=True) * (1.0 / WIDTH)
         result = inv[k][0:1] * (grad_hat - first - standard * second)
-        grad[2 * k], grad[2 * k + 1] = rows_of(result)
-        keep(turn, k, result, pad_g)
+        keep(turn, k, result)
         for which, term in ((0, dot_nt(normed, grad_pre)), (1, dot_nt(grad_branch, value))):
             for part in range(3):
                 sums[which, part, :WIDTH, :] += term[:, SPAN * part : SPAN * (part + 1)]
@@ -385,11 +415,11 @@
 
     over_chunks(late)
     send_lines(2)
-    depth_terms(pad_two, True)
+    depth_terms(1, 2, True)
     edge_depth(2, 1, True)
-    depthwise(pad_g, conv, True)
-    take_rows(2, pad_g)
-    depthwise_ends(pad_g, conv, True)
+    depthwise(2, True)
+    take_rows(2)
+    depthwise_ends(2, True)
     take_lines(2, 2, True)
 
     def early(k):
@@ -440,7 +470,7 @@
     for d in (1, 2, 3, 0):
         half_out[line_at(d)] = sums[1 - core, line_at(d)].astype(BF16)
         halves[d].start()
-    depth_terms(pad_one, False, 0, 6)
+    depth_terms(0, 3, False, 0, 3)
 
     for d in (1, 2, 3):
         halves[d].wait_recv()
@@ -448,7 +478,7 @@
         quarters[d - 1].start()
     halves[0].wait_recv()
     slot_sum[...] = sums[core, x_at] + half_in[x_at].astype(F32)
-    depth_terms(pad_one, False, 6, BLOCKS)
+    depth_terms(0, 3, False, 3, BLOCKS)
 
     for copy in quarters:
         copy.wait_recv()
@@ -459,17 +489,17 @@
         owner(member_at(d))(lambda d=d: slot_copy(d).start())
 
     edge_depth(3, 0, False)
-    column = lax.broadcasted_iota(jnp.int32, (WIDTH, COLS), 1)
-    picked = jnp.zeros((WIDTH, COLS), F32)
+    column = lax.broadcasted_iota(jnp.int32, (FULL, COLS), 1)
+    picked = jnp.zeros((FULL, COLS), F32)
     for t in range(49):
         picked = jnp.where(column == t, jnp.sum(depth_acc[t], axis=1, keepdims=True), picked)
-    turned = jnp.concatenate([picked, jnp.zeros((56, COLS), F32)], axis=0).T[:64] + edge_terms[...]
+    turned = jnp.concatenate([picked, jnp.zeros((48, COLS), F32)], axis=0).T[:64] + edge_terms[...]
     for piece in range(16):
         depth_own[piece] = turned[
             8 * (piece // 2) : 8 * (piece // 2) + 8, COLS * (piece % 2) : COLS * (piece % 2) + COLS]
     for d in range(1, 16):
         depth_copy(d).start()
-    depthwise(pad_g, conv, True, 0, 10)
+    depthwise(3, True, 0, 5)
 
     @pl.when(member < 13)
     def _():
@@ -490,7 +520,7 @@
     depth_mid[...] = total
     for d in range(1, 8):
         peer_copy(d).start()
-    depthwise(pad_g, conv, True, 10, BLOCKS)
+    depthwise(3, True, 5, BLOCKS)
 
     for d in range(1, 16):
         owner(member_at(16 - d))(lambda d=d: done_copy(d).wait_recv())
@@ -504,8 +534,8 @@
     depth_all[member] = total * scale
     for d in range(1, 16):
         spread_copy(d).start()
-    take_rows(3, pad_g)
-    depthwise_ends(pad_g, conv, True)
+    take_rows(3)
+    depthwise_ends(3, True)
     take_lines(3, 2, True)
 
     def last(k):
@@ -546,22 +576,21 @@
 
 def main_call(scale, *operands):
     vmem = pl.BlockSpec(memory_space=pltpu.VMEM)
-    padded = pltpu.VMEM((14, WIDTH, COLS), F32)
     plane = pltpu.VMEM((ROWS, WIDTH, COLS), F32)
     tile = (8, COLS)
     return pl.pallas_call(
-        functools.partial(main_kernel, scale),
+        functools.partial(staged_kernel, scale),
         out_shape=[
             jax.ShapeDtypeStruct((LEVELS * ROWS, COLS), F32),
             jax.ShapeDtypeStruct((2, 4, 208, SPAN), BF16),
             jax.ShapeDtypeStruct((7, 7, WIDTH), F32),
         ],
-        in_specs=[vmem] * len(operands),
+        in_specs=[pl.BlockSpec(memory_space=pl.ANY)] * len(operands),
         out_specs=[vmem] * 3,
         scratch_shapes=[
-            pltpu.VMEM((49, WIDTH, COLS), F32),
-            padded, padded, padded,
-            plane, plane, plane, plane,
+            pltpu.VMEM((49, FULL, COLS), BF16),
+            pltpu.VMEM((ROWS, FULL, COLS), F32),
+            plane, plane,
             pltpu.VMEM((CHUNKS, 8, SPAN), F32),
             pltpu.VMEM((CHUNKS, 8, SPAN), F32),
             pltpu.VMEM((CHUNKS, HIDDEN, SPAN), BF16),
@@ -570,7 +599,7 @@
             pltpu.VMEM((CHUNKS, WIDTH, SPAN), BF16),
             pltpu.VMEM((CHUNKS, WIDTH, SPAN), F32),
             pltpu.VMEM((CHUNKS, LEVELS, SPAN), F32),
-            pltpu.VMEM((49, WIDTH, COLS), F32),
+            pltpu.VMEM((49, FULL, COLS), F32),
             pltpu.VMEM((HIDDEN, WIDTH), BF16),
             pltpu.VMEM((HIDDEN, WIDTH), BF16),
             pltpu.VMEM((LEVELS, WIDTH), BF16),
@@ -582,7 +611,7 @@
             pltpu.SemaphoreType.DMA((4, 10)),
             pltpu.SemaphoreType.DMA((4, 10)),
             pltpu.VMEM((128, SPAN), F32),
-            pltpu.VMEM((WIDTH, COLS), F32),
+            pltpu.VMEM((FULL, COLS), F32),
             pltpu.VMEM((2, 4, 208, SPAN), F32),
             pltpu.VMEM((4, 208, SPAN), BF16),
             pltpu.VMEM((4, 208, SPAN), BF16),
@@ -602,6 +631,8 @@
             pltpu.VMEM((3, 6, 16, SPAN), F32),
             pltpu.VMEM((WIDTH, COLS), BF16),
             pltpu.VMEM((64, SPAN), F32),
+            *[pltpu.VMEM(value.shape, value.dtype) for value in operands],
+            pltpu.SemaphoreType.DMA((INPUTS,)),
         ],
         compiler_params=pltpu.CompilerParams(
             collective_id=0, has_side_effects=True, vmem_limit_bytes=58 * 1024 * 1024),

time: 85.2 us -> 78.7 us (0.924)
  Pallas kernels: 84.4 us -> 77.9 us
    pallas_call x1, Pallas kernels: 81.9 us -> 75.3 us  [main_call(): pl.pallas_call(functools.partial(staged_kernel, scale), out_shape=[jax.Sh...]
where the time goes in v3:
time: 78.7 us; the launch traced here: 78.5 us
  Pallas kernels  77.9 us (99%)
    pallas_call x1, Pallas kernels, main_call(): pl.pallas_call(functools.partial(staged_kernel, scale), out_shape=[jax.Sh...  75.3 us
    pallas_call x1, Pallas kernels, result_call(): pl.pallas_call(result_kernel, out_shape=[jax.ShapeDtypeStruct((LEVELS * R...  2.57 us

profile of v3, /device:TPU:1, one launch (start us, length us, event | category | flops | bytes accessed | tf_op | source)
XLA Modules:
  0.0 78.5 jit_solution(5149537751987567487)
XLA Ops:
  0.6 75.3 %shard_map.147 = (f32[800,128]{1,0:T(8,128)}, bf16[2,4,208,256]{3,2,1,0:T(8,128)(2,1)}, f32[7,7,200]{2,1,0:T(8,128)}) custom-call(f32[800,128]{1,0:T(8,128)} %bitcast.10, s32[8,128]{1,0:T(8,128)} %refs_1_.1, f32[800,128]{1,0:T(8,128)} %bitcast.11, bf16[200,100]{1,0:T(8,128)(2,1)} %refs_3_.1, f32[1,200]{1,0:T(1,128)} %bitcast.15, f32[7,7,200]{2,1,0:T(8,128)} %bitcast.13, ...), custom_call_target="tpu_custom_call" | custom-call | tf_op jit(solution)/shard_map/pallas_call | solution.py:581
  75.9 2.6 %shard_map.148 = (f32[800,128]{1,0:T(8,128)}, f32[200,800]{1,0:T(8,128)}, f32[200,800]{1,0:T(8,128)}, f32[7,7,200]{2,1,0:T(8,128)}) custom-call(f32[800,128]{1,0:T(8,128)} %get-tuple-element.11.state, bf16[2,4,208,256]{3,2,1,0:T(8,128)(2,1)} %get-tuple-element.12.gathered, f32[7,7,200]{2,1,0:T(8,128)} %get-tuple-element.13.depth), custom_call_target="tpu_custom_call" | custom-call | tf_op jit(solution)/shard_map/pallas_call | solution.py:654

commit v4 on v3

--- a/solution.py
+++ b/solution.py
@@ -467,12 +467,12 @@
     def owner(index):
         return lambda run: pl.when(index < 13)(run)
 
-    for d in (1, 2, 3, 0):
+    for d in (2, 1, 3, 0):
         half_out[line_at(d)] = sums[1 - core, line_at(d)].astype(BF16)
         halves[d].start()
     depth_terms(0, 3, False, 0, 3)
 
-    for d in (1, 2, 3):
+    for d in (2, 1, 3):
         halves[d].wait_recv()
         quarter_out[line_at(d)] = (sums[core, line_at(d)] + half_in[line_at(d)].astype(F32)).astype(BF16)
         quarters[d - 1].start()
@@ -524,7 +524,7 @@
 
     for d in range(1, 16):
         owner(member_at(16 - d))(lambda d=d: done_copy(d).wait_recv())
-    for d in range(1, 4):
+    for d in (2, 1, 3):
         line_copy(d).start()
     backs[0].start()
     total = depth_mid[...]
@@ -545,7 +545,7 @@
             out[pl.ds(2 * k + q, LEVELS, stride=ROWS), :] = result[:, COLS * q : COLS * (q + 1)]
 
     over_chunks(last)
-    for d in (1, 2, 3):
+    for d in (1, 3, 2):
         line_copy(d).wait_recv()
         backs[4 - d].start()
     for d in range(1, 16):

time: 78.7 us -> 78.1 us (level)
  no operation moved by 1% of the time
where the time goes in v4:
time: 78.1 us; the launch traced here: 77.9 us
  Pallas kernels  77.3 us (99%)
    pallas_call x1, Pallas kernels, main_call(): pl.pallas_call(functools.partial(staged_kernel, scale), out_shape=[jax.Sh...  74.7 us
    pallas_call x1, Pallas kernels, result_call(): pl.pallas_call(result_kernel, out_shape=[jax.ShapeDtypeStruct((LEVELS * R...  2.57 us

profile of v4, /device:TPU:1, one launch (start us, length us, event | category | flops | bytes accessed | tf_op | source)
XLA Modules:
  0.0 77.9 jit_solution(13767543152825044307)
XLA Ops:
  0.6 74.7 %shard_map.147 = (f32[800,128]{1,0:T(8,128)}, bf16[2,4,208,256]{3,2,1,0:T(8,128)(2,1)}, f32[7,7,200]{2,1,0:T(8,128)}) custom-call(f32[800,128]{1,0:T(8,128)} %bitcast.10, s32[8,128]{1,0:T(8,128)} %refs_1_.1, f32[800,128]{1,0:T(8,128)} %bitcast.11, bf16[200,100]{1,0:T(8,128)(2,1)} %refs_3_.1, f32[1,200]{1,0:T(1,128)} %bitcast.15, f32[7,7,200]{2,1,0:T(8,128)} %bitcast.13, ...), custom_call_target="tpu_custom_call" | custom-call | tf_op jit(solution)/shard_map/pallas_call | solution.py:581
  75.3 2.6 %shard_map.148 = (f32[800,128]{1,0:T(8,128)}, f32[200,800]{1,0:T(8,128)}, f32[200,800]{1,0:T(8,128)}, f32[7,7,200]{2,1,0:T(8,128)}) custom-call(f32[800,128]{1,0:T(8,128)} %get-tuple-element.11.state, bf16[2,4,208,256]{3,2,1,0:T(8,128)(2,1)} %get-tuple-element.12.gathered, f32[7,7,200]{2,1,0:T(8,128)} %get-tuple-element.13.depth), custom_call_target="tpu_custom_call" | custom-call | tf_op jit(solution)/shard_map/pallas_call | solution.py:654
